TPU v7x, 256 devices: a whole 4x4x8 slice. The times are simulated.
256 devices in a mesh: sec: 2 (over z_lo), band: 32 (over y, x, core), fld: 4 (over z_hi).
Axes of the slice: x: 4, y: 4, z: 8 (z_hi: 4, z_lo: 2; z = z_hi * 2 + z_lo), core: 2. Of those that a mesh axis runs over, the one named last changes fastest.
Arguments:
- grid: bfloat16 [4, 16, 1280, 2688], P('fld', 'sec', 'band'), may hold values from -6 to 6
- legendre: bfloat16 [768, 1280, 768], P(('band', 'fld'), None, 'sec'), may hold values from -0.15625 to 0.15625
- counts: int32 [32], replicated, may hold values from 1 to 1024, 16384 in all
- blocks: int32 [32768], P('band'), may hold values from 0 to 839
- interp: bfloat16 [32768, 128], P('band'), may hold values from -0.5 to 0.5
- source_weights: bfloat16 [64, 2048], replicated, may hold values from -0.75 to 0.75
- inverses: bfloat16 [64, 32, 32], replicated, may hold values from -1 to 1
Outputs:
- spectral: bfloat16 [768, 2, 4, 16, 768], P(('band', 'fld'), None, None, None, 'sec')
- heating: bfloat16 [16, 1280, 2688], P(('sec', 'fld'), 'band')
Inputs may be any that keep to these rules, and one draw needn't show every extreme that they name: Band b has counts[b] live slots, slots 0 to counts[b] - 1; the counts sum to 16384 and the largest is 1024.
All inputs are finite; a program needn't handle non-finite values.
Results may differ from a plain program's by a relative error of at most 0.0085.
Values may be sent and summed in bfloat16 or wider, within the bound.
A program may use at most 64 MiB of HBM per device.

v0:
```python
import math

import jax
import jax.numpy as jnp
from jax import lax
from jax.sharding import PartitionSpec as P


def dft_table(lon, waves):
    column = jnp.arange(2 * waves, dtype=jnp.int32)
    wave = column // 2
    part = column % 2
    place = jnp.arange(lon, dtype=jnp.int32)
    phase = place[:, None] * wave[None, :] % lon
    angle = phase.astype(jnp.float32) * (2.0 * math.pi / lon)
    values = jnp.where(part[None, :] == 0, jnp.cos(angle), -jnp.sin(angle))
    return (values * (1.0 / math.sqrt(lon))).astype(jnp.bfloat16)


def heat_rates(flux, count, start):
    levels = flux.shape[0] // 2
    width = flux.shape[1]
    upward = flux[:levels]
    downward = flux[levels:]
    empty = jnp.zeros((1, width), jnp.float32)
    up_next = jnp.concatenate([upward[1:], empty], axis=0)
    down_next = jnp.concatenate([downward[1:], empty], axis=0)
    heat = upward - up_next - (downward - down_next)
    slots = start + jnp.arange(width, dtype=jnp.int32)
    heat = jnp.where(slots[None, :] < count, heat, jnp.zeros_like(heat))
    return heat.astype(jnp.bfloat16)


def body(grid, legendre, counts, blocks, interp, source_weights, inverses):
    n_sec = lax.axis_size("sec")
    n_band = lax.axis_size("band")
    n_fld = lax.axis_size("fld")
    lev_s = grid.shape[1]
    lat_d = grid.shape[2]
    lon = grid.shape[3]
    wave_dev = legendre.shape[0]
    degrees = legendre.shape[2]
    waves = wave_dev * n_band * n_fld
    groups = n_sec * n_fld
    flat_rows = grid.reshape(lev_s * lat_d, lon)
    table = dft_table(lon, waves)
    coeffs = jnp.dot(flat_rows, table, preferred_element_type=jnp.float32).astype(jnp.bfloat16)
    coeffs = coeffs.reshape(1, 1, lev_s, lat_d, n_band, n_fld, 2 * wave_dev)
    moved = lax.all_to_all(
        lax.all_to_all(coeffs, "band", split_axis=4, concat_axis=0, tiled=True),
        "fld",
        split_axis=5,
        concat_axis=1,
        tiled=True,
    )
    moved = moved.reshape(n_band, n_fld, lev_s, lat_d, wave_dev, 2)
    levels_all = lax.all_gather(moved, "sec", axis=2, tiled=True)
    weights = legendre.reshape(wave_dev, n_band, lat_d, degrees)
    spectral = jnp.einsum(
        "bflakr,kban->krfln", levels_all, weights, preferred_element_type=jnp.float32
    )
    spectral = spectral.astype(jnp.bfloat16)
    slots_all = blocks.shape[0]
    width = interp.shape[1]
    nblocks = lat_d * lon // width
    patch = grid.reshape(lev_s, nblocks, width)
    block_ids = jnp.arange(nblocks, dtype=jnp.int32)
    selector = (blocks[:, None] == block_ids[None, :]).astype(jnp.bfloat16)
    picked = lax.dot_general(
        selector, patch, (((1,), (1,)), ((), ())), preferred_element_type=jnp.float32
    )
    picked = picked.astype(jnp.bfloat16)
    partial_state = jnp.einsum("jlk,jk->lj", picked, interp, preferred_element_type=jnp.float32)
    partial_state = partial_state.astype(jnp.bfloat16).reshape(1, lev_s, slots_all)
    columns = lax.all_to_all(partial_state, ("sec", "fld"), split_axis=2, concat_axis=0, tiled=True)
    per_dev = slots_all // groups
    state = columns.reshape(n_sec, n_fld, lev_s, per_dev)
    state = jnp.transpose(state, (1, 0, 2, 3)).reshape(n_fld * n_sec * lev_s, per_dev)
    gates = lax.dot_general(
        source_weights, state, (((0,), (0,)), ((), ())), preferred_element_type=jnp.float32
    )
    spec_bands = inverses.shape[0]
    flux_rows = inverses.shape[1]
    source = jax.nn.softplus(gates).astype(jnp.bfloat16).reshape(spec_bands, flux_rows, per_dev)
    flux = jnp.einsum("bpq,bqj->pj", inverses, source, preferred_element_type=jnp.float32)
    band_place = lax.axis_index("band")
    count = jnp.sum(
        jnp.where(jnp.arange(n_band, dtype=jnp.int32) == band_place, counts, jnp.zeros_like(counts))
    )
    group_place = lax.axis_index(("sec", "fld"))
    heat = heat_rates(flux, count, group_place * per_dev)
    returned = lax.all_to_all(heat, ("sec", "fld"), split_axis=0, concat_axis=1, tiled=True)
    spread = (
        jnp.transpose(returned.astype(jnp.float32))[:, :, None]
        * interp.astype(jnp.float32)[:, None, :]
    )
    spread_high = spread.astype(jnp.bfloat16)
    spread_low = (spread - spread_high.astype(jnp.float32)).astype(jnp.bfloat16)
    summed = lax.dot_general(
        selector, spread_high, (((0,), (0,)), ((), ())), preferred_element_type=jnp.float32
    )
    summed = summed + lax.dot_general(
        selector, spread_low, (((0,), (0,)), ((), ())), preferred_element_type=jnp.float32
    )
    heating = (
        jnp.transpose(summed, (1, 0, 2)).reshape(returned.shape[0], lat_d, lon).astype(jnp.bfloat16)
    )
    return (spectral, heating)


def solution(mesh):
    return jax.shard_map(
        body,
        mesh=mesh,
        in_specs=(
            P("fld", "sec", "band", None),
            P(("band", "fld"), None, "sec"),
            P(),
            P("band"),
            P("band", None),
            P(),
            P(),
        ),
        out_specs=(P(("band", "fld"), None, None, None, "sec"), P(("sec", "fld"), "band", None)),
        check_vma=False,
    )
```

profile of v0, /device:TPU:32, one launch (start us, length us, event | category | flops | bytes accessed | tf_op | source)
XLA Modules:
  0.0 271.1 jit_solution(12231743176324524661)
XLA Ops:
  7.2 0.0 copy-start
  7.2 74.4 %fusion.15 = bf16[320,1536]{1,0:T(8,128)(2,1)S(1)} fusion(bf16[320,2688]{1,0:T(8,128)(2,1)} %bitcast.111, s32[1536]{0:T(1024)S(1)} %add_select_fusion.1, pred[1536]{0:T(1024)(128)(4,1)S(1)} %fusion.44), kind=kOutput, calls=%fused_computation.17 | convolution fusion | flops 2696577024 | bytes 2711040 | tf_op jit(solution)/shard_map/dot_general | solution.py:47
  81.6 1.4 copy.42
  83.0 4.3 %reshape.74 = bf16[1,1,8,40,32,4,12]{3,2,6,5,4,1,0:T(8,128)(2,1)S(1)} reshape(bf16[320,1536]{0,1:T(8,128)(2,1)} %copy.42) | data formatting | bytes 1966080 | tf_op jit(solution)/shard_map/reshape | solution.py:48
  87.2 1.9 bitcast_bitcast_fusion.2
  89.1 6.9 %reshape.89 = bf16[32,2,7680]{2,1,0:T(2,128)(2,1)S(1)} reshape(bf16[32,1,1,4,12,8,40]{6,5,4,3,2,1,0:T(8,128)(2,1)} %bitcast_bitcast_fusion.2) | data formatting | bytes 1966080
  96.0 23.9 %all_to_all.61 = bf16[32,2,7680]{2,1,0:T(2,128)(2,1)} all-to-all(bf16[32,2,7680]{2,1,0:T(2,128)(2,1)S(1)} %reshape.89), channel_id=1, replica_groups=mesh['sec'=2,'band'=32,'fld'=4] {'band'}, dimensions={0} | all-to-all | bytes 1966080 | tf_op jit(solution)/shard_map/all_to_all | solution.py:50
  119.9 7.1 %reshape.90 = bf16[32,1,1,4,12,8,40]{6,5,4,3,2,1,0:T(8,128)(2,1)S(1)} reshape(bf16[32,2,7680]{2,1,0:T(2,128)(2,1)} %all_to_all.61) | data formatting | bytes 1966080
  127.0 1.9 copy_bitcast_fusion
  129.0 0.0 copy-start.1
  129.0 6.7 %reshape.91 = bf16[4,2,61440]{2,1,0:T(2,128)(2,1)} reshape(bf16[4,1,1,32,12,8,40]{6,5,4,3,2,1,0:T(8,128)(2,1)} %copy_bitcast_fusion) | data formatting | bytes 1966080
  135.6 0.0 copy-start.5
  135.6 7.7 %all-to-all-start.1 = ((bf16[4,2,61440]{2,1,0:T(2,128)(2,1)}), bf16[4,2,61440]{2,1,0:T(2,128)(2,1)}, u32[]{:S(2)}, u32[]{:S(2)}) async-start(bf16[4,2,61440]{2,1,0:T(2,128)(2,1)} %reshape.91), calls=%async_computation.1 | async-start | bytes 1966080 | tf_op jit(solution)/shard_map/all_to_all | solution.py:49
  143.3 0.0 all-gather.2.cloned.1.call-start
  143.3 0.0 copy-done.1
  143.3 3.0 %reshape.77 = bf16[8,840,128]{2,1,0:T(8,128)(2,1)} reshape(bf16[1,8,40,2688]{3,2,1,0:T(8,128)(2,1)S(1)} %copy-done.1) | data formatting | bytes 3440640 | tf_op jit(solution)/shard_map/reshape | solution.py:66
  146.3 0.0 copy-done.5
  146.3 0.0 copy-start.3
  146.3 3.9 %fusion.18 = bf16[1024,8,128]{2,0,1:T(8,128)(2,1)S(1)} fusion(bf16[8,840,128]{2,1,0:T(8,128)(2,1)} %reshape.77, s32[1024]{0:T(1024)S(1)} %copy-done.5), kind=kOutput, calls=%fused_computation.21 | convolution fusion | flops 1763516416 | bytes 3821568 | tf_op jit(solution)/shard_map/dot_general | solution.py:69
  150.2 0.0 copy-done.3
  150.2 1.6 fusion.16
  151.8 0.2 copy.58
  152.1 18.5 %all-to-all-done.1 = bf16[4,2,61440]{2,1,0:T(2,128)(2,1)} async-done(((bf16[4,2,61440]{2,1,0:T(2,128)(2,1)}), bf16[4,2,61440]{2,1,0:T(2,128)(2,1)}, u32[]{:S(2)}, u32[]{:S(2)}) %all-to-all-start.1) | async-done | bytes 983072 | tf_op jit(solution)/shard_map/all_to_all | solution.py:49
  170.6 5.7 %reshape.92 = bf16[4,1,1,32,12,8,40]{6,5,4,3,2,1,0:T(8,128)(2,1)S(1)} reshape(bf16[4,2,61440]{2,1,0:T(2,128)(2,1)} %all-to-all-done.1) | data formatting | bytes 1966080
  176.3 2.6 copy.46
  178.9 0.0 copy-start.6
  178.9 0.0 copy-start.2
  178.9 0.0 all-gather.2.cloned.1.call-update
  178.9 0.4 copy.47
  179.3 0.5 broadcast.73
  179.8 2.3 reduce
  182.1 0.0 copy-start.4
  182.1 0.9 reshape.93
  183.0 4.3 %all-to-all-start.2 = ((bf16[8,2,512]{2,1,0:T(2,128)(2,1)}), bf16[8,2,512]{2,1,0:T(2,128)(2,1)S(1)}, u32[]{:S(2)}, u32[]{:S(2)}) async-start(bf16[8,2,512]{2,1,0:T(2,128)(2,1)} %reshape.93), calls=%async_computation.2 | async-start | bytes 32768 | tf_op jit(solution)/shard_map/all_to_all | solution.py:75
  187.3 0.0 copy-done.6
  187.3 0.6 fusion.53
  187.9 0.7 add_compare_fusion
  188.6 0.0 copy-done.2
  188.6 0.8 copy.52
  189.4 4.3 %all-to-all-done.2 = bf16[8,2,512]{2,1,0:T(2,128)(2,1)S(1)} async-done(((bf16[8,2,512]{2,1,0:T(2,128)(2,1)}), bf16[8,2,512]{2,1,0:T(2,128)(2,1)S(1)}, u32[]{:S(2)}, u32[]{:S(2)}) %all-to-all-start.2) | async-done | bytes 16416 | tf_op jit(solution)/shard_map/all_to_all | solution.py:75
  193.7 0.7 reshape.94
  194.4 0.3 copy.48
  194.7 0.0 copy-done
  194.7 0.7 fusion.36
  195.4 0.3 copy.51
  195.7 0.3 convolution_bitcast_fusion.2
  196.1 0.6 fusion.48
  196.7 4.6 %all-to-all-start.3 = ((bf16[8,2,128]{2,1,0:T(2,128)(2,1)}), bf16[8,2,128]{2,1,0:T(2,128)(2,1)S(1)}, u32[]{:S(2)}, u32[]{:S(2)}) async-start(bf16[8,2,128]{2,1,0:T(2,128)(2,1)} %bitcast.30), calls=%async_computation.3 | async-start | bytes 8192 | tf_op jit(solution)/shard_map/all_to_all | solution.py:92
  201.4 0.0 copy-done.4
  201.4 6.1 %all-to-all-done.3 = bf16[8,2,128]{2,1,0:T(2,128)(2,1)S(1)} async-done(((bf16[8,2,128]{2,1,0:T(2,128)(2,1)}), bf16[8,2,128]{2,1,0:T(2,128)(2,1)S(1)}, u32[]{:S(2)}, u32[]{:S(2)}) %all-to-all-start.3) | async-done | bytes 4128 | tf_op jit(solution)/shard_map/all_to_all | solution.py:92
  207.5 0.8 fusion.8
  208.4 0.9 fusion.32
  209.3 1.2 convert_element_type.81
  210.5 46.8 %all-gather.2.cloned.1.call-done = bf16[32,4,16,40,6,2]{3,2,0,5,1,4:T(8,128)(2,1)} async-done(((bf16[32,4,8,40,6,2]{3,2,0,5,1,4:T(8,128)(2,1)}), bf16[32,4,16,40,6,2]{3,2,0,5,1,4:T(8,128)(2,1)}) %all-gather.2.cloned.1.call-update) | async-done | bytes 1966096 | tf_op jit(solution)/shard_map/all_gather | solution.py:57
  257.3 6.0 %fusion.31 = bf16[6,2,4,16,384]{4,3,1,2,0:T(8,128)(2,1)S(1)} fusion(bf16[32,4,16,40,6,2]{3,2,0,5,1,4:T(8,128)(2,1)} %all-gather.2.cloned.1.call-done, bf16[6,32,40,384,1,1]{3,2,1,5,4,0:T(8,128)(2,1)} %bitcast.117), kind=kOutput, calls=%fused_computation.31 | convolution fusion | flops 755269632 | bytes 8454144 | tf_op jit(solution)/shard_map/bflakr,kban->krfln/dot_general | solution.py:59
  263.3 0.9 copy.53
  (9 shorter events, 0.1 us)
Async XLA Ops:
  7.2 187.5 %copy-start = (bf16[64,2048]{1,0:T(8,128)(2,1)S(1)}, bf16[64,2048]{1,0:T(8,128)(2,1)}, u32[]{:S(2)}) copy-start(bf16[64,2048]{1,0:T(8,128)(2,1)} %param.12) | copy-start | bytes 786436
  129.0 14.4 %copy-start.1 = (bf16[1,8,40,2688]{3,2,1,0:T(8,128)(2,1)S(1)}, bf16[1,8,40,2688]{3,2,1,0:T(8,128)(2,1)}, u32[]{:S(2)}) copy-start(bf16[1,8,40,2688]{3,2,1,0:T(8,128)(2,1)} %param.7) | copy-start | bytes 5160964
  135.6 10.7 %copy-start.5 = (s32[1024]{0:T(1024)S(1)}, s32[1024]{0:T(1024)}, u32[]{:S(2)}) copy-start(s32[1024]{0:T(1024)} %param.10) | copy-start | bytes 12292
  135.6 35.0 %all-to-all-start.1 = ((bf16[4,2,61440]{2,1,0:T(2,128)(2,1)}), bf16[4,2,61440]{2,1,0:T(2,128)(2,1)}, u32[]{:S(2)}, u32[]{:S(2)}) async-start(bf16[4,2,61440]{2,1,0:T(2,128)(2,1)} %reshape.91), calls=%async_computation.1 | async-start | bytes 1966080 | tf_op jit(solution)/shard_map/all_to_all | solution.py:49
  143.3 114.0 %all-gather.2.cloned.1.call-start = ((), (), s32[]{:S(2)}) async-start(), calls=%async_computation.4 | async-start | bytes 9437184 | tf_op jit(solution)/shard_map/all_gather | solution.py:57
  146.3 3.9 %copy-start.3 = (bf16[1024,128]{1,0:T(8,128)(2,1)S(1)}, bf16[1024,128]{1,0:T(8,128)(2,1)}, u32[]{:S(2)}) copy-start(bf16[1024,128]{1,0:T(8,128)(2,1)} %param.11) | copy-start | bytes 786436
  178.9 8.4 %copy-start.6 = (s32[32]{0:T(128)S(1)}, s32[32]{0:T(128)}, u32[]{:S(2)}) copy-start(s32[32]{0:T(128)} %param.9) | copy-start | bytes 388
  178.9 9.7 %copy-start.2 = (bf16[64,32,32]{0,2,1:T(8,128)(2,1)S(1)}, bf16[64,32,32]{0,2,1:T(8,128)(2,1)}, u32[]{:S(2)}) copy-start(bf16[64,32,32]{0,2,1:T(8,128)(2,1)} %param.13) | copy-start | bytes 393220
  182.1 19.3 %copy-start.4 = (bf16[1024,128]{1,0:T(8,128)(2,1)S(1)}, bf16[1024,128]{1,0:T(8,128)(2,1)}, u32[]{:S(2)}) copy-start(bf16[1024,128]{1,0:T(8,128)(2,1)} %param.11) | copy-start | bytes 786436
  183.0 10.7 %all-to-all-start.2 = ((bf16[8,2,512]{2,1,0:T(2,128)(2,1)}), bf16[8,2,512]{2,1,0:T(2,128)(2,1)S(1)}, u32[]{:S(2)}, u32[]{:S(2)}) async-start(bf16[8,2,512]{2,1,0:T(2,128)(2,1)} %reshape.93), calls=%async_computation.2 | async-start | bytes 32768 | tf_op jit(solution)/shard_map/all_to_all | solution.py:75
  196.7 10.8 %all-to-all-start.3 = ((bf16[8,2,128]{2,1,0:T(2,128)(2,1)}), bf16[8,2,128]{2,1,0:T(2,128)(2,1)S(1)}, u32[]{:S(2)}, u32[]{:S(2)}) async-start(bf16[8,2,128]{2,1,0:T(2,128)(2,1)} %bitcast.30), calls=%async_computation.3 | async-start | bytes 8192 | tf_op jit(solution)/shard_map/all_to_all | solution.py:92
Sparse Core Ops, SparseCore 0:
  179.0 78.2 all-gather.1
where the time goes:
time: 274 us; the launch traced here: 271 us
  matrix products  88.7 us (32%)
  waiting for transfers between devices  75.7 us (28%)
  local copies, waits for them, and re-layouts  47.6 us (17%)
  blocking collectives  23.9 us (9%)
  starting transfers between devices  16.7 us (6%)
  between operations  14.2 us (5%)
  other arithmetic  4.25 us (2%)
    dot_general x1, matrix products, body(): jnp.dot(flat_rows, table, preferred_element_type=jnp.float32)  74.4 us
    all_gather x1, waiting for transfers between devices, body(): levels_all = lax.all_gather(moved, 'sec', axis=2, tiled=True)  46.8 us
    unnamed x26, local copies, waits for them, and re-layouts  34 us
    all_to_all x1, blocking collectives, body(): lax.all_to_all(coeffs, 'band', split_axis=4, concat_axis=0, tiled=True)  23.9 us
    all_to_all x1, waiting for transfers between devices, body(): lax.all_to_all(lax.all_to_all(coeffs, 'band', split_axis=4, concat_axis=0...  18.5 us
    all_to_all x1, starting transfers between devices, body(): lax.all_to_all(lax.all_to_all(coeffs, 'band', split_axis=4, concat_axis=0...  7.69 us
    all_to_all x1, waiting for transfers between devices, body(): lax.all_to_all(heat, ('sec', 'fld'), split_axis=0, concat_axis=1, tiled=T...  6.1 us
    dot_general x1, matrix products, body(): jnp.einsum('bflakr,kban->krfln', levels_all, weights, preferred_element_t...  6.03 us
  transfers between devices with their start and end apart: 4, of which 4 were waited for; matrix products, arithmetic and copies ran while one was open for 8% of the time, Pallas kernels for 0%

commit v1 on v0

--- a/solution.py
+++ b/solution.py
@@ -1,20 +1,261 @@
+import functools
 import math
 
 import jax
 import jax.numpy as jnp
+import ml_dtypes
+import numpy as np
 from jax import lax
+from jax.experimental import pallas as pl
+from jax.experimental.pallas import tpu as pltpu
 from jax.sharding import PartitionSpec as P
 
-
-def dft_table(lon, waves):
-    column = jnp.arange(2 * waves, dtype=jnp.int32)
-    wave = column // 2
-    part = column % 2
-    place = jnp.arange(lon, dtype=jnp.int32)
-    phase = place[:, None] * wave[None, :] % lon
-    angle = phase.astype(jnp.float32) * (2.0 * math.pi / lon)
-    values = jnp.where(part[None, :] == 0, jnp.cos(angle), -jnp.sin(angle))
-    return (values * (1.0 / math.sqrt(lon))).astype(jnp.bfloat16)
+MESH = pl.DeviceIdType.MESH
+N_BAND = 32
+N_Z = 8
+CHUNKS = 3
+
+
+def dft_table(lon, wave_dev, n_fld):
+    waves = wave_dev * N_BAND * n_fld
+    per_chunk = wave_dev // CHUNKS
+    place = np.arange(lon, dtype=np.int64)
+    wave = np.zeros((CHUNKS, 2, 2, n_fld, per_chunk, 2, 8), np.int64)
+    part = np.zeros_like(wave)
+    c, h, t, f, m, r, i = np.indices(wave.shape)
+    band = (h * 2 + t) * 8 + i
+    wave = (band * n_fld + f) * wave_dev + c * per_chunk + m
+    part = r
+    wave = wave.reshape(CHUNKS * 2, 256)
+    part = part.reshape(CHUNKS * 2, 256)
+    phase = (place[None, :, None] * wave[:, None, :]) % lon
+    angle = phase.astype(np.float32) * np.float32(2.0 * math.pi / lon)
+    values = np.where(part[:, None, :] == 0, np.cos(angle), -np.sin(angle))
+    return (values.astype(np.float32) * np.float32(1.0 / math.sqrt(lon))).astype(ml_dtypes.bfloat16)
+
+
+def transpose_levels(rows):
+    lane = lax.broadcasted_iota(jnp.int32, rows[0].shape, 1)
+    for bit in (1, 2, 4):
+        high = (lane & bit) != 0
+        out = list(rows)
+        for l in range(8):
+            if l & bit:
+                continue
+            a, b = rows[l], rows[l + bit]
+            out[l] = jnp.where(high, pltpu.roll(b, bit, 1), a)
+            out[l + bit] = jnp.where(high, b, pltpu.roll(a, 128 - bit, 1))
+        rows = out
+    return rows
+
+
+def kernel(
+    grid_hbm, tab_hbm, leg_hbm, out_ref,
+    g, tab, leg, send, recv, zsend, zrecv,
+    load_sem, bs_sem, br_sem, zs_sem, zr_sem, rs_sem, rr_sem,
+):
+    lat = send.shape[2]
+    band = lax.axis_index("band")
+    z = lax.axis_index("fld") * 2 + lax.axis_index("sec")
+    sign = 1 - 2 * lax.rem(z, 2)
+
+    def zdev(step):
+        at = lax.rem(z + step + 2 * N_Z, N_Z)
+        return at, {"sec": lax.rem(at, 2), "fld": at // 2}
+
+    partner, partner_dev = zdev(sign)
+
+    def load_tab(t):
+        return pltpu.make_async_copy(tab_hbm.at[t], tab.at[t], load_sem.at[t])
+
+    def load_leg(c):
+        return pltpu.make_async_copy(
+            leg_hbm.at[pl.ds(2 * c, 2)], leg.at[pl.ds(2 * c, 2)], load_sem.at[7 + c]
+        )
+
+    half0 = band // 16
+    load_g = pltpu.make_async_copy(grid_hbm, g, load_sem.at[6])
+    load_g.start()
+    load_tab(half0).start()
+
+    barrier = pltpu.get_barrier_semaphore()
+
+    def greet(k, _):
+        pl.semaphore_signal(
+            barrier, inc=1, device_id={"band": lax.rem(band + k, N_BAND)}, device_id_type=MESH
+        )
+        return 0
+
+    lax.fori_loop(1, N_BAND, greet, 0)
+    for d in range(1, N_Z):
+        pl.semaphore_signal(barrier, inc=1, device_id=zdev(d)[1], device_id_type=MESH)
+    load_g.wait()
+    pl.semaphore_wait(barrier, N_BAND - 1 + N_Z - 1)
+
+    def band_copy(c, to):
+        return pltpu.make_async_remote_copy(
+            src_ref=send.at[c, to],
+            dst_ref=recv.at[c, band],
+            send_sem=bs_sem.at[c],
+            recv_sem=br_sem.at[c],
+            device_id={"band": to},
+            device_id_type=MESH,
+        )
+
+    def table_of(t):
+        return (t // 2) * 2 + lax.rem(t + half0, 2)
+
+    def dft_step(t, _):
+        c = t // 2
+        half = lax.rem(t + half0, 2)
+
+        @pl.when(t < 5)
+        def _():
+            load_tab(table_of(t + 1)).start()
+
+        load_tab(table_of(t)).wait()
+        coeffs = jnp.dot(g[...], tab[table_of(t)], preferred_element_type=jnp.float32)
+        for tile in range(2):
+            rows = [coeffs[l * lat:(l + 1) * lat, tile * 128:(tile + 1) * 128] for l in range(8)]
+            rows = transpose_levels(rows)
+            for i in range(8):
+                send[c, half * 16 + tile * 8 + i] = rows[i].astype(jnp.bfloat16)
+
+        def send_one(k, _):
+            to = half * 16 + lax.rem(band + k, 16)
+
+            @pl.when(to != band)
+            def _():
+                band_copy(c, to).start()
+
+            return 0
+
+        lax.fori_loop(0, 16, send_one, 0)
+        return 0
+
+    lax.fori_loop(0, 2 * CHUNKS, dft_step, 0)
+    for c in range(CHUNKS):
+        load_leg(c).start()
+
+    row = lax.broadcasted_iota(jnp.int32, (128, 128), 0)
+    col = lax.broadcasted_iota(jnp.int32, (128, 128), 1)
+    eye = (row == col).astype(jnp.bfloat16)
+
+    def own_copy(c):
+        return pltpu.make_async_remote_copy(
+            src_ref=zsend.at[c, z // 2], dst_ref=zrecv.at[c, z],
+            send_sem=zs_sem.at[c, 0], recv_sem=zr_sem.at[c, 0],
+            device_id=partner_dev, device_id_type=MESH,
+        )
+
+    def direct_copy(c, d):
+        at, dev = zdev({1: -sign, 2: 2 * sign, 3: -3 * sign}[d])
+        return pltpu.make_async_remote_copy(
+            src_ref=zsend.at[c, at // 2], dst_ref=zrecv.at[c, z],
+            send_sem=zs_sem.at[c, d], recv_sem=zr_sem.at[c, d],
+            device_id=dev, device_id_type=MESH,
+        )
+
+    def relay_copy(c, d):
+        source, _ = zdev(-d * sign)
+        return pltpu.make_async_remote_copy(
+            src_ref=zrecv.at[c, source], dst_ref=zrecv.at[c, source],
+            send_sem=rs_sem.at[c, d - 1], recv_sem=rr_sem.at[c, d - 1],
+            device_id=partner_dev, device_id_type=MESH,
+        )
+
+    def turn(c):
+        recv[c, band] = send[c, band]
+        got = recv.at[c, pl.ds(0, N_BAND - 1)]
+        pltpu.make_async_copy(got, got, br_sem.at[c]).wait()
+        half = N_BAND // 2
+        for part in range(2):
+            rows = recv[c, part * half:(part + 1) * half].astype(jnp.float32).reshape(half * lat, 128)
+            turned = lax.dot_general(
+                eye, rows.astype(jnp.bfloat16), (((1,), (1,)), ((), ())),
+                preferred_element_type=jnp.float32,
+            ).astype(jnp.bfloat16)
+            zsend[c, :, :, part * half * lat:(part + 1) * half * lat] = turned.reshape(4, 32, half * lat)
+        for d in (3, 2, 1):
+            direct_copy(c, d).start()
+        own_copy(c).start()
+        zrecv[c, z] = zsend[c, z // 2]
+
+    def relay(c):
+        for d in (1, 2, 3):
+            direct_copy(c, d).wait_recv()
+            relay_copy(c, d).start()
+
+    def legendre(c):
+        own_copy(c).wait_recv()
+        for d in (1, 2, 3):
+            relay_copy(c, d).wait_recv()
+        load_leg(c).wait()
+
+        def one(m, _):
+            rows = pl.ds(pl.multiple_of(m * 16, 16), 16)
+            data = zrecv[c, :, rows, :].reshape(128, zrecv.shape[3])
+            out = jnp.dot(data, leg[2 * c + m], preferred_element_type=jnp.float32)
+            out = out.reshape(4, 2, 2, 8, out.shape[1])
+            for r in range(2):
+                for f in range(4):
+                    both = jnp.concatenate([out[f, 0, r], out[f, 1, r]], axis=0)
+                    out_ref[2 * c + m, r, f] = both.astype(jnp.bfloat16)
+            return 0
+
+        lax.fori_loop(0, 2, one, 0)
+
+    turn(0)
+    turn(1)
+    relay(0)
+    turn(2)
+    relay(1)
+    legendre(0)
+    relay(2)
+    legendre(1)
+    legendre(2)
+
+    for c in range(CHUNKS):
+        sent = send.at[c, pl.ds(0, N_BAND - 1)]
+        pltpu.make_async_copy(sent, sent, bs_sem.at[c]).wait()
+        own_copy(c).wait_send()
+        for d in (1, 2, 3):
+            direct_copy(c, d).wait_send()
+            relay_copy(c, d).wait_send()
+
+
+def spectral_part(grid, legendre):
+    lev_s, lat_d, lon = grid.shape[1:]
+    wave_dev, lats, degrees = legendre.shape
+    n_fld = lax.axis_size("fld")
+    table = jnp.asarray(dft_table(lon, wave_dev, n_fld))
+    flat = grid.reshape(lev_s * lat_d, lon)
+    bf16 = jnp.bfloat16
+    return pl.pallas_call(
+        kernel,
+        out_shape=jax.ShapeDtypeStruct((wave_dev, 2, n_fld, 2 * lev_s, degrees), bf16),
+        in_specs=[pl.BlockSpec(memory_space=pl.ANY)] * 3,
+        out_specs=pl.BlockSpec(memory_space=pltpu.VMEM),
+        scratch_shapes=[
+            pltpu.VMEM(flat.shape, bf16),
+            pltpu.VMEM(table.shape, bf16),
+            pltpu.VMEM(legendre.shape, bf16),
+            pltpu.VMEM((CHUNKS, N_BAND, lat_d, 128), bf16),
+            pltpu.VMEM((CHUNKS, N_BAND, lat_d, 128), bf16),
+            pltpu.VMEM((CHUNKS, n_fld, 32, lats), bf16),
+            pltpu.VMEM((CHUNKS, N_Z, 32, lats), bf16),
+            pltpu.SemaphoreType.DMA((10,)),
+            pltpu.SemaphoreType.DMA((CHUNKS,)),
+            pltpu.SemaphoreType.DMA((CHUNKS,)),
+            pltpu.SemaphoreType.DMA((CHUNKS, 4)),
+            pltpu.SemaphoreType.DMA((CHUNKS, 4)),
+            pltpu.SemaphoreType.DMA((CHUNKS, 3)),
+            pltpu.SemaphoreType.DMA((CHUNKS, 3)),
+        ],
+        compiler_params=pltpu.CompilerParams(
+            collective_id=0, has_side_effects=True, vmem_limit_bytes=48 * 2**20
+        ),
+    )(flat, table, legendre)
 
 
 def heat_rates(flux, count, start):
@@ -31,35 +272,14 @@
     return heat.astype(jnp.bfloat16)
 
 
-def body(grid, legendre, counts, blocks, interp, source_weights, inverses):
+def heating_part(grid, counts, blocks, interp, source_weights, inverses):
     n_sec = lax.axis_size("sec")
     n_band = lax.axis_size("band")
     n_fld = lax.axis_size("fld")
     lev_s = grid.shape[1]
     lat_d = grid.shape[2]
     lon = grid.shape[3]
-    wave_dev = legendre.shape[0]
-    degrees = legendre.shape[2]
-    waves = wave_dev * n_band * n_fld
     groups = n_sec * n_fld
-    flat_rows = grid.reshape(lev_s * lat_d, lon)
-    table = dft_table(lon, waves)
-    coeffs = jnp.dot(flat_rows, table, preferred_element_type=jnp.float32).astype(jnp.bfloat16)
-    coeffs = coeffs.reshape(1, 1, lev_s, lat_d, n_band, n_fld, 2 * wave_dev)
-    moved = lax.all_to_all(
-        lax.all_to_all(coeffs, "band", split_axis=4, concat_axis=0, tiled=True),
-        "fld",
-        split_axis=5,
-        concat_axis=1,
-        tiled=True,
-    )
-    moved = moved.reshape(n_band, n_fld, lev_s, lat_d, wave_dev, 2)
-    levels_all = lax.all_gather(moved, "sec", axis=2, tiled=True)
-    weights = legendre.reshape(wave_dev, n_band, lat_d, degrees)
-    spectral = jnp.einsum(
-        "bflakr,kban->krfln", levels_all, weights, preferred_element_type=jnp.float32
-    )
-    spectral = spectral.astype(jnp.bfloat16)
     slots_all = blocks.shape[0]
     width = interp.shape[1]
     nblocks = lat_d * lon // width
@@ -102,9 +322,12 @@
     summed = summed + lax.dot_general(
         selector, spread_low, (((0,), (0,)), ((), ())), preferred_element_type=jnp.float32
     )
-    heating = (
-        jnp.transpose(summed, (1, 0, 2)).reshape(returned.shape[0], lat_d, lon).astype(jnp.bfloat16)
-    )
+    return jnp.transpose(summed, (1, 0, 2)).reshape(returned.shape[0], lat_d, lon).astype(jnp.bfloat16)
+
+
+def body(grid, legendre, counts, blocks, interp, source_weights, inverses):
+    spectral = spectral_part(grid, legendre)
+    heating = heating_part(grid, counts, blocks, interp, source_weights, inverses)
     return (spectral, heating)
 
 

time: 274 us -> 95.2 us (0.35)
  matrix products: 88.7 us -> 6.79 us
  waiting for transfers between devices: 75.7 us -> 3.69 us
  Pallas kernels: 0 us -> 53.2 us
  local copies, waits for them, and re-layouts: 47.6 us -> 9.79 us
  blocking collectives: 23.9 us -> 0 us
  between operations: 14.2 us -> 0.87 us
  starting transfers between devices: 16.7 us -> 13.2 us
    dot_general x8 -> x6, matrix products: 88.7 us -> 6.79 us  [the longest x1 2.39 us: heating_part(): lax.dot_general(selector, patch, (((1,), (1,)), ((), ())), preferred_elem...]
    pallas_call x0 -> x1, Pallas kernels: none -> 53.2 us  [spectral_part(): pl.pallas_call(kernel, out_shape=jax.ShapeDtypeStruct((wave_dev, 2, n_fld...]
    all_gather x1 -> x0, waiting for transfers between devices: 46.8 us -> none  [body(): levels_all = lax.all_gather(moved, 'sec', axis=2, tiled=True)]
    unnamed x26 -> x20, local copies, waits for them, and re-layouts: 34 us -> 3.72 us
    all_to_all x3 -> x2, waiting for transfers between devices: 28.9 us -> 3.69 us  [the longest x1 3.69 us: heating_part(): lax.all_to_all(partial_state, ('sec', 'fld'), split_axis=2, concat_axis=0...]
    all_to_all x1 -> x0, blocking collectives: 23.9 us -> none  [body(): lax.all_to_all(coeffs, 'band', split_axis=4, concat_axis=0, tiled=True)]
    reshape x5 -> x3, local copies, waits for them, and re-layouts: 10.2 us -> 4.01 us  [the longest x1 3.62 us: heating_part(): patch = grid.reshape(lev_s, nblocks, width)]
    all_to_all x3 -> x2, starting transfers between devices: 16.7 us -> 13.2 us  [the longest x1 8.57 us: heating_part(): lax.all_to_all(partial_state, ('sec', 'fld'), split_axis=2, concat_axis=0...]
  transfers between devices with their start and end apart: 4 -> 2, of which waited for: 4 -> 1; matrix products, arithmetic and copies ran while one was open for 8% -> 4% of each run, Pallas kernels for 0% -> 57%
where the time goes in v1:
time: 95.2 us; the launch traced here: 94 us
  Pallas kernels  53.2 us (56%)
  starting transfers between devices  13.2 us (14%)
  local copies, waits for them, and re-layouts  9.79 us (10%)
  matrix products  6.79 us (7%)
  other arithmetic  6.44 us (7%)
  waiting for transfers between devices  3.69 us (4%)
    pallas_call x1, Pallas kernels, spectral_part(): pl.pallas_call(kernel, out_shape=jax.ShapeDtypeStruct((wave_dev, 2, n_fld...  53.2 us
    all_to_all x1, starting transfers between devices, heating_part(): lax.all_to_all(partial_state, ('sec', 'fld'), split_axis=2, concat_axis=0...  8.57 us
    all_to_all x1, starting transfers between devices, heating_part(): lax.all_to_all(heat, ('sec', 'fld'), split_axis=0, concat_axis=1, tiled=T...  4.59 us
    unnamed x20, local copies, waits for them, and re-layouts  3.72 us
    all_to_all x1, waiting for transfers between devices, heating_part(): lax.all_to_all(partial_state, ('sec', 'fld'), split_axis=2, concat_axis=0...  3.69 us
    reshape x1, local copies, waits for them, and re-layouts, heating_part(): patch = grid.reshape(lev_s, nblocks, width)  3.62 us
    dot_general x1, matrix products, heating_part(): lax.dot_general(selector, patch, (((1,), (1,)), ((), ())), preferred_elem...  2.39 us
    unnamed x1, other arithmetic  2.27 us
  transfers between devices with their start and end apart: 2, of which 1 were waited for; matrix products, arithmetic and copies ran while one was open for 4% of the time, Pallas kernels for 57%

profile of v1, /device:TPU:32, one launch (start us, length us, event | category | flops | bytes accessed | tf_op | source)
XLA Modules:
  0.0 94.0 jit_solution(6287797496249482617)
XLA Ops:
  0.6 0.0 copy-start
  0.6 0.0 copy-start.4
  0.7 3.6 %reshape.40 = bf16[8,840,128]{2,1,0:T(8,128)(2,1)S(1)} reshape(bf16[1,8,40,2688]{3,2,1,0:T(8,128)(2,1)} %param.8) | data formatting | bytes 3440640 | tf_op jit(solution)/shard_map/reshape | solution.py:286
  4.3 0.0 copy-done.4
  4.3 0.0 copy-start.3
  4.3 2.4 %fusion.9 = bf16[1024,8,128]{2,0,1:T(8,128)(2,1)S(1)} fusion(bf16[8,840,128]{2,1,0:T(8,128)(2,1)S(1)} %reshape.40, s32[1024]{0:T(1024)S(1)} %copy-done.4), kind=kOutput, calls=%fused_computation.9 | convolution fusion | flops 1763516416 | bytes 3821568 | tf_op jit(solution)/shard_map/dot_general | solution.py:289
  6.7 0.0 copy-done.3
  6.7 1.6 %fusion.7 = bf16[1024,1,8]{2,1,0:T(2,128)(2,1)S(1)} fusion(bf16[1024,8,128]{2,0,1:T(8,128)(2,1)S(1)} %fusion.9, bf16[1024,128,1]{1,0,2:T(8,128)(2,1)S(1)} %bitcast.67), kind=kOutput, calls=%fused_computation.7 | convolution fusion | flops 2097152 | bytes 2375680 | tf_op jit(solution)/shard_map/jlk,jk->lj/dot_general | solution.py:293
  8.3 0.0 copy-start.6
  8.3 0.0 copy-start.2
  8.3 0.3 copy.35
  8.6 0.4 copy.27
  9.0 0.5 broadcast.16
  9.5 2.3 %reduce = bf16[1024,8]{1,0:T(8,128)(2,1)S(1)} reduce(bf16[1024,1,8]{2,1,0:T(2,128)(2,1)S(1)} %bitcast.64, bf16[]{:T(256)} %broadcast.16), dimensions={1}, to_apply=%bitcast.54.reduce_sub_computation | reduce | bytes 32770
  11.8 0.9 reshape.50
  12.7 8.6 %all-to-all-start = ((bf16[8,2,512]{2,1,0:T(2,128)(2,1)}), bf16[8,2,512]{2,1,0:T(2,128)(2,1)S(1)}, u32[]{:S(2)}, u32[]{:S(2)}) async-start(bf16[8,2,512]{2,1,0:T(2,128)(2,1)} %reshape.50), calls=%async_computation | async-start | bytes 32768 | tf_op jit(solution)/shard_map/all_to_all | solution.py:295
  21.2 0.0 copy-done.6
  21.2 0.6 fusion.36
  21.9 1.2 %add_compare_fusion = pred[128]{0:T(512)(128)(4,1)} fusion(s32[]{:T(128)} %fusion.36, s32[]{:T(128)S(6)} %mul.20), kind=kLoop, calls=%fused_computation.37 | loop fusion | flops 256 | bytes 136 | tf_op jit(solution)/shard_map/lt | solution.py:271
  23.1 0.0 copy-done.2
  23.1 0.8 copy.32
  23.9 3.7 %all-to-all-done = bf16[8,2,512]{2,1,0:T(2,128)(2,1)S(1)} async-done(((bf16[8,2,512]{2,1,0:T(2,128)(2,1)}), bf16[8,2,512]{2,1,0:T(2,128)(2,1)S(1)}, u32[]{:S(2)}, u32[]{:S(2)}) %all-to-all-start) | async-done | bytes 16416 | tf_op jit(solution)/shard_map/all_to_all | solution.py:295
  27.6 0.7 reshape.51
  28.3 0.3 copy.28
  28.6 0.0 copy-done
  28.6 0.0 copy-start.1
  28.6 0.8 fusion.25
  29.4 0.3 copy.31
  29.6 0.3 convolution_bitcast_fusion.1
  30.0 1.3 %fusion.35 = bf16[16,128]{1,0:T(8,128)(2,1)} fusion(f32[32,128]{1,0:T(8,128)S(1)} %convolution_bitcast_fusion.1, f32[15,128]{1,0:T(8,128)S(1)} %get-tuple-element.3, f32[15,128]{1,0:T(8,128)S(1)} %get-tuple-element.2, pred[128]{0:T(512)(128)(4,1)} %add_compare_fusion), kind=kLoop, calls=%fused_computation.32 | loop fusion | flops 10240 | bytes 35968 | tf_op jit(solution)/shard_map/convert_element_type | solution.py:272
  31.3 4.6 %all-to-all-start.1 = ((bf16[8,2,128]{2,1,0:T(2,128)(2,1)}), bf16[8,2,128]{2,1,0:T(2,128)(2,1)S(1)}, u32[]{:S(2)}, u32[]{:S(2)}) async-start(bf16[8,2,128]{2,1,0:T(2,128)(2,1)} %bitcast.15), calls=%async_computation.1 | async-start | bytes 8192 | tf_op jit(solution)/shard_map/all_to_all | solution.py:312
  35.9 1.0 %convert_element_type.51 = f32[1024,128]{1,0:T(8,128)S(1)} convert(bf16[1024,128]{1,0:T(8,128)(2,1)} %param.12) | non-fusion elementwise | flops 131072 | bytes 786432 | tf_op jit(solution)/shard_map/convert_element_type | solution.py:315
  36.9 0.0 copy-done.1
  36.9 0.0 copy-start.5
  36.9 53.2 %shard_map.95 = bf16[6,2,4,16,384]{4,3,2,1,0:T(8,128)(2,1)S(1)} custom-call(bf16[320,2688]{1,0:T(8,128)(2,1)S(1)} %bitcast.63, bf16[6,2688,256]{2,1,0:T(8,128)(2,1)} %constant.29.clone.tab_hbm, bf16[6,1280,384]{2,1,0:T(8,128)(2,1)} %leg_hbm.1), custom_call_target="tpu_custom_call" | custom-call | tf_op jit(solution)/shard_map/pallas_call | solution.py:234
  90.1 0.0 all-to-all-done.1
  90.2 0.0 copy-done.5
  90.2 0.8 fusion.1
  91.0 0.9 fusion.21
  91.9 1.2 %convert_element_type.57 = bf16[2,40,2688]{2,1,0:T(8,128)(2,1)} reshape(bf16[2,840,128]{2,1,0:T(8,128)(2,1)S(1)} %fusion.21) | data formatting | bytes 860160 | tf_op jit(solution)/shard_map/convert_element_type | solution.py:325
  93.1 0.8 copy.44
  (6 shorter events, 0.1 us)
Async XLA Ops:
  0.6 27.9 %copy-start = (bf16[64,2048]{1,0:T(8,128)(2,1)S(1)}, bf16[64,2048]{1,0:T(8,128)(2,1)}, u32[]{:S(2)}) copy-start(bf16[64,2048]{1,0:T(8,128)(2,1)} %param.13) | copy-start | bytes 786436
  0.6 3.6 %copy-start.4 = (s32[1024]{0:T(1024)S(1)}, s32[1024]{0:T(1024)}, u32[]{:S(2)}) copy-start(s32[1024]{0:T(1024)} %param.11) | copy-start | bytes 12292
  4.3 2.4 %copy-start.3 = (bf16[1024,128]{1,0:T(8,128)(2,1)S(1)}, bf16[1024,128]{1,0:T(8,128)(2,1)}, u32[]{:S(2)}) copy-start(bf16[1024,128]{1,0:T(8,128)(2,1)} %param.12) | copy-start | bytes 786436
  8.3 12.9 %copy-start.6 = (s32[32]{0:T(128)S(1)}, s32[32]{0:T(128)}, u32[]{:S(2)}) copy-start(s32[32]{0:T(128)} %param.10) | copy-start | bytes 388
  8.3 14.8 %copy-start.2 = (bf16[64,32,32]{0,2,1:T(8,128)(2,1)S(1)}, bf16[64,32,32]{0,2,1:T(8,128)(2,1)}, u32[]{:S(2)}) copy-start(bf16[64,32,32]{0,2,1:T(8,128)(2,1)} %param.14) | copy-start | bytes 393220
  12.7 14.9 %all-to-all-start = ((bf16[8,2,512]{2,1,0:T(2,128)(2,1)}), bf16[8,2,512]{2,1,0:T(2,128)(2,1)S(1)}, u32[]{:S(2)}, u32[]{:S(2)}) async-start(bf16[8,2,512]{2,1,0:T(2,128)(2,1)} %reshape.50), calls=%async_computation | async-start | bytes 32768 | tf_op jit(solution)/shard_map/all_to_all | solution.py:295
  28.6 8.3 %copy-start.1 = (bf16[1,8,40,2688]{3,2,1,0:T(8,128)(2,1)S(1)}, bf16[1,8,40,2688]{3,2,1,0:T(8,128)(2,1)}, u32[]{:S(2)}) copy-start(bf16[1,8,40,2688]{3,2,1,0:T(8,128)(2,1)} %param.8) | copy-start | bytes 5160964
  31.3 58.8 %all-to-all-start.1 = ((bf16[8,2,128]{2,1,0:T(2,128)(2,1)}), bf16[8,2,128]{2,1,0:T(2,128)(2,1)S(1)}, u32[]{:S(2)}, u32[]{:S(2)}) async-start(bf16[8,2,128]{2,1,0:T(2,128)(2,1)} %bitcast.15), calls=%async_computation.1 | async-start | bytes 8192 | tf_op jit(solution)/shard_map/all_to_all | solution.py:312
  36.9 53.3 %copy-start.5 = (s32[1024]{0:T(1024)S(1)}, s32[1024]{0:T(1024)}, u32[]{:S(2)}) copy-start(s32[1024]{0:T(1024)} %param.11) | copy-start | bytes 12292

commit v2 on v1

--- a/solution.py
+++ b/solution.py
@@ -14,6 +14,7 @@
 N_BAND = 32
 N_Z = 8
 CHUNKS = 3
+PATCH_ROWS = 896
 
 
 def dft_table(lon, wave_dev, n_fld):
@@ -50,9 +51,12 @@
 
 
 def kernel(
-    grid_hbm, tab_hbm, leg_hbm, out_ref,
+    grid_hbm, tab_hbm, leg_hbm, counts_hbm, blocks_hbm, interp_hbm, weights_hbm, inverse_hbm,
+    out_ref, heat_ref,
     g, tab, leg, send, recv, zsend, zrecv,
-    load_sem, bs_sem, br_sem, zs_sem, zr_sem, rs_sem, rr_sem,
+    counts, blocks, interp, weights, inverse,
+    ids, patch, inverse_wide, source, state_send, state_recv, heat_send, heat_recv,
+    load_sem, bs_sem, br_sem, zs_sem, zr_sem, rs_sem, rr_sem, small_sem, col_sem,
 ):
     lat = send.shape[2]
     band = lax.axis_index("band")
@@ -134,6 +138,15 @@
         return 0
 
     lax.fori_loop(0, 2 * CHUNKS, dft_step, 0)
+    small = [
+        pltpu.make_async_copy(source_ref, target_ref, small_sem.at[i])
+        for i, (source_ref, target_ref) in enumerate(
+            ((blocks_hbm, blocks), (interp_hbm, interp), (weights_hbm, weights),
+             (inverse_hbm, inverse), (counts_hbm, counts))
+        )
+    ]
+    for load in small:
+        load.start()
     for c in range(CHUNKS):
         load_leg(c).start()
 
@@ -205,16 +218,181 @@
 
         lax.fori_loop(0, 2, one, 0)
 
+    n_tiles = g.shape[1] // 128
+    pairs = (n_tiles + 1) // 2
+    pair_rows = 2 * lat
+
+    def block_patch():
+        def tile_rows(t):
+            cols = pl.ds(pl.multiple_of(t * 128, 128), 128)
+            return g[:, cols].astype(jnp.float32)
+
+        def put(u, first, second):
+            rows = pl.ds(pl.multiple_of(u * pair_rows, 16), pair_rows)
+            for l in range(8):
+                span = slice(l * lat, (l + 1) * lat)
+                both = jnp.concatenate([first[span], second[span]], axis=0)
+                patch[rows, l * 128:(l + 1) * 128] = both.astype(jnp.bfloat16)
+
+        def one(u, _):
+            put(u, tile_rows(2 * u), tile_rows(2 * u + 1))
+            return 0
+
+        lax.fori_loop(0, n_tiles // 2, one, 0)
+        if n_tiles % 2:
+            last = tile_rows(n_tiles - 1)
+            put(n_tiles // 2, last, jnp.zeros_like(last))
+        end = pairs * pair_rows
+        patch[end:, :] = jnp.zeros((PATCH_ROWS - end, patch.shape[1]), jnp.bfloat16)
+        small[0].wait()
+        chosen = blocks[...].astype(jnp.float32)
+        at_lat = jnp.floor((chosen + 0.5) * (1.0 / n_tiles))
+        ids[...] = (chosen - at_lat * n_tiles) * lat + at_lat
+
+    def column_copy(kind, to, from_buf, to_buf):
+        return pltpu.make_async_remote_copy(
+            src_ref=from_buf.at[to], dst_ref=to_buf.at[z],
+            send_sem=col_sem.at[2 * kind], recv_sem=col_sem.at[2 * kind + 1],
+            device_id={"sec": lax.rem(to, 2), "fld": to // 2}, device_id_type=MESH,
+        )
+
+    def column_wait(kind, is_recv, buf):
+        part = buf.at[pl.ds(0, N_Z - 1)]
+        pltpu.make_async_copy(part, part, col_sem.at[2 * kind + is_recv]).wait()
+
+    def gather_state():
+        small[1].wait()
+        lane = lax.broadcasted_iota(jnp.int32, (128, 128), 1)
+        level_of = lax.broadcasted_iota(jnp.int32, (8, 1024), 1) // 128
+        ones = (lax.broadcasted_iota(jnp.int32, (8, 1024), 0) == level_of).astype(jnp.bfloat16)
+
+        def one(k, _):
+            to = lax.rem(z + k, N_Z)
+            want = jnp.transpose(jnp.broadcast_to(ids[pl.ds(to, 1), :], (128, 128)))
+            hot = jnp.concatenate(
+                [(want == (lane + 128 * i).astype(jnp.float32)).astype(jnp.bfloat16)
+                 for i in range(PATCH_ROWS // 128)],
+                axis=1,
+            )
+            picked = jnp.dot(hot, patch[...], preferred_element_type=jnp.float32)
+            slot = pl.ds(pl.multiple_of(to * 128, 128), 128)
+            factor = interp[slot, :].astype(jnp.float32)
+            terms = picked * jnp.concatenate([factor] * 8, axis=1)
+            high = terms.astype(jnp.bfloat16)
+            low = (terms - high.astype(jnp.float32)).astype(jnp.bfloat16)
+            contract = (((1,), (1,)), ((), ()))
+            state_send[to] = lax.dot_general(
+                ones, high, contract, preferred_element_type=jnp.float32
+            ) + lax.dot_general(ones, low, contract, preferred_element_type=jnp.float32)
+
+            @pl.when(to != z)
+            def _():
+                column_copy(0, to, state_send, state_recv).start()
+
+            return 0
+
+        lax.fori_loop(1, N_Z + 1, one, 0)
+
+    def solve_columns():
+        small[2].wait()
+        small[3].wait()
+        small[4].wait()
+        inverse_wide[...] = inverse[...].astype(jnp.float32)
+        state_recv[z] = state_send[z]
+        column_wait(0, 1, state_recv)
+        state = state_recv[...].reshape(64, 128).astype(jnp.bfloat16)
+
+        def sources(i, _):
+            cols = pl.ds(pl.multiple_of(i * 256, 256), 256)
+            gates = lax.dot_general(
+                weights[:, cols], state, (((0,), (0,)), ((), ())), preferred_element_type=jnp.float32
+            )
+            source[cols, :] = jax.nn.softplus(gates)
+            return 0
+
+        lax.fori_loop(0, weights.shape[1] // 256, sources, 0)
+        spec_bands = inverse.shape[1]
+        flux_rows = inverse.shape[0] // 32
+
+        def fluxes(q, total):
+            factor = inverse_wide[pl.ds(q, 32, stride=32), :].astype(jnp.bfloat16)
+            value = source[pl.ds(q, spec_bands, stride=32), :].astype(jnp.bfloat16)
+            return total + jnp.dot(factor, value, preferred_element_type=jnp.float32)
+
+        flux = lax.fori_loop(0, flux_rows, fluxes, jnp.zeros((32, 128), jnp.float32))
+        row16 = lax.broadcasted_iota(jnp.int32, (16, 128), 0)
+
+        def drop(rows):
+            above = jnp.where(row16 < 15, pltpu.roll(rows, 15, 0), 0.0)
+            return rows - above
+
+        heat = drop(flux[:16]) - drop(flux[16:])
+        slot = (z * 128 + lax.broadcasted_iota(jnp.int32, (1, 128), 1)).astype(jnp.float32)
+        at = lax.broadcasted_iota(jnp.int32, (1, N_BAND), 1)
+        live = jnp.sum(
+            jnp.where(at == band, counts[...].astype(jnp.float32), 0.0), axis=1, keepdims=True
+        )
+        heat = jnp.where(slot < live, heat, 0.0)
+        heat = heat.astype(jnp.bfloat16).astype(jnp.float32)
+        for group in range(N_Z):
+            rows = heat[(group // 4) * 8:(group // 4) * 8 + 8]
+            shift = (8 - 2 * (group % 4)) % 8
+            heat_send[2 * (group % 4) + group // 4] = pltpu.roll(rows, shift, 0) if shift else rows
+
+        def send_heat(k, _):
+            column_copy(1, lax.rem(z + k, N_Z), heat_send, heat_recv).start()
+            return 0
+
+        lax.fori_loop(1, N_Z, send_heat, 0)
+
+    def scatter_heat():
+        heat_recv[z] = heat_send[z]
+        column_wait(1, 1, heat_recv)
+        step = lax.broadcasted_iota(jnp.int32, (pair_rows, 128), 0)
+
+        def one(u, _):
+            row = (step + u * pair_rows).astype(jnp.float32)
+            parts = [[], []]
+            for place in range(N_Z):
+                hit = ids[place:place + 1, :] == row
+                for l in range(2):
+                    parts[l].append(
+                        jnp.where(hit, heat_recv[place, l:l + 1, :], 0.0).astype(jnp.bfloat16)
+                    )
+            rows = jnp.concatenate([jnp.concatenate(p, axis=1) for p in parts], axis=0)
+            summed = jnp.dot(rows, interp[...], preferred_element_type=jnp.float32)
+            for l in range(2):
+                for t in range(2):
+                    value = summed[l * pair_rows + t * lat:l * pair_rows + (t + 1) * lat]
+                    cols = pl.ds(pl.multiple_of((2 * u + t) * 128, 128), 128)
+
+                    def put():
+                        heat_ref[l, :, cols] = value.astype(jnp.bfloat16)
+
+                    if t == 0:
+                        put()
+                    else:
+                        pl.when(2 * u + 1 < n_tiles)(put)
+            return 0
+
+        lax.fori_loop(0, pairs, one, 0)
+
     turn(0)
+    block_patch()
     turn(1)
+    gather_state()
     relay(0)
     turn(2)
+    solve_columns()
     relay(1)
     legendre(0)
+    scatter_heat()
     relay(2)
     legendre(1)
     legendre(2)
 
+    column_wait(0, 0, state_send)
+    column_wait(1, 0, heat_send)
     for c in range(CHUNKS):
         sent = send.at[c, pl.ds(0, N_BAND - 1)]
         pltpu.make_async_copy(sent, sent, bs_sem.at[c]).wait()
@@ -224,18 +402,30 @@
             relay_copy(c, d).wait_send()
 
 
-def spectral_part(grid, legendre):
+def body(grid, legendre, counts, blocks, interp, source_weights, inverses):
     lev_s, lat_d, lon = grid.shape[1:]
     wave_dev, lats, degrees = legendre.shape
     n_fld = lax.axis_size("fld")
+    n_sec = lax.axis_size("sec")
+    slots, width = interp.shape
+    rows_in, sources = source_weights.shape
+    spec_bands, flux_rows, _ = inverses.shape
     table = jnp.asarray(dft_table(lon, wave_dev, n_fld))
     flat = grid.reshape(lev_s * lat_d, lon)
-    bf16 = jnp.bfloat16
-    return pl.pallas_call(
+    inv_rows = jnp.transpose(inverses, (1, 2, 0)).reshape(flux_rows * flux_rows, spec_bands)
+    lev_out = n_sec * lev_s // (n_sec * n_fld)
+    bf16, f32 = jnp.bfloat16, jnp.float32
+    spectral, heating = pl.pallas_call(
         kernel,
-        out_shape=jax.ShapeDtypeStruct((wave_dev, 2, n_fld, 2 * lev_s, degrees), bf16),
-        in_specs=[pl.BlockSpec(memory_space=pl.ANY)] * 3,
-        out_specs=pl.BlockSpec(memory_space=pltpu.VMEM),
+        out_shape=(
+            jax.ShapeDtypeStruct((wave_dev, 2, n_fld, n_sec * lev_s, degrees), bf16),
+            jax.ShapeDtypeStruct((lev_out, lat_d, lon), bf16),
+        ),
+        in_specs=[pl.BlockSpec(memory_space=pl.ANY)] * 8,
+        out_specs=(
+            pl.BlockSpec(memory_space=pltpu.VMEM),
+            pl.BlockSpec(memory_space=pltpu.VMEM),
+        ),
         scratch_shapes=[
             pltpu.VMEM(flat.shape, bf16),
             pltpu.VMEM(table.shape, bf16),
@@ -244,6 +434,19 @@
             pltpu.VMEM((CHUNKS, N_BAND, lat_d, 128), bf16),
             pltpu.VMEM((CHUNKS, n_fld, 32, lats), bf16),
             pltpu.VMEM((CHUNKS, N_Z, 32, lats), bf16),
+            pltpu.VMEM((1, N_BAND), jnp.int32),
+            pltpu.VMEM((N_Z, 128), jnp.int32),
+            pltpu.VMEM(interp.shape, bf16),
+            pltpu.VMEM(source_weights.shape, bf16),
+            pltpu.VMEM(inv_rows.shape, bf16),
+            pltpu.VMEM((N_Z, 128), f32),
+            pltpu.VMEM((PATCH_ROWS, lev_s * width), bf16),
+            pltpu.VMEM(inv_rows.shape, f32),
+            pltpu.VMEM((sources, 128), f32),
+            pltpu.VMEM((N_Z, 8, 128), f32),
+            pltpu.VMEM((N_Z, 8, 128), f32),
+            pltpu.VMEM((N_Z, 8, 128), f32),
+            pltpu.VMEM((N_Z, 8, 128), f32),
             pltpu.SemaphoreType.DMA((10,)),
             pltpu.SemaphoreType.DMA((CHUNKS,)),
             pltpu.SemaphoreType.DMA((CHUNKS,)),
@@ -251,83 +454,16 @@
             pltpu.SemaphoreType.DMA((CHUNKS, 4)),
             pltpu.SemaphoreType.DMA((CHUNKS, 3)),
             pltpu.SemaphoreType.DMA((CHUNKS, 3)),
+            pltpu.SemaphoreType.DMA((5,)),
+            pltpu.SemaphoreType.DMA((4,)),
         ],
         compiler_params=pltpu.CompilerParams(
             collective_id=0, has_side_effects=True, vmem_limit_bytes=48 * 2**20
         ),
-    )(flat, table, legendre)
-
-
-def heat_rates(flux, count, start):
-    levels = flux.shape[0] // 2
-    width = flux.shape[1]
-    upward = flux[:levels]
-    downward = flux[levels:]
-    empty = jnp.zeros((1, width), jnp.float32)
-    up_next = jnp.concatenate([upward[1:], empty], axis=0)
-    down_next = jnp.concatenate([downward[1:], empty], axis=0)
-    heat = upward - up_next - (downward - down_next)
-    slots = start + jnp.arange(width, dtype=jnp.int32)
-    heat = jnp.where(slots[None, :] < count, heat, jnp.zeros_like(heat))
-    return heat.astype(jnp.bfloat16)
-
-
-def heating_part(grid, counts, blocks, interp, source_weights, inverses):
-    n_sec = lax.axis_size("sec")
-    n_band = lax.axis_size("band")
-    n_fld = lax.axis_size("fld")
-    lev_s = grid.shape[1]
-    lat_d = grid.shape[2]
-    lon = grid.shape[3]
-    groups = n_sec * n_fld
-    slots_all = blocks.shape[0]
-    width = interp.shape[1]
-    nblocks = lat_d * lon // width
-    patch = grid.reshape(lev_s, nblocks, width)
-    block_ids = jnp.arange(nblocks, dtype=jnp.int32)
-    selector = (blocks[:, None] == block_ids[None, :]).astype(jnp.bfloat16)
-    picked = lax.dot_general(
-        selector, patch, (((1,), (1,)), ((), ())), preferred_element_type=jnp.float32
+    )(
+        flat, table, legendre, counts.reshape(1, N_BAND), blocks.reshape(N_Z, 128), interp,
+        source_weights, inv_rows,
     )
-    picked = picked.astype(jnp.bfloat16)
-    partial_state = jnp.einsum("jlk,jk->lj", picked, interp, preferred_element_type=jnp.float32)
-    partial_state = partial_state.astype(jnp.bfloat16).reshape(1, lev_s, slots_all)
-    columns = lax.all_to_all(partial_state, ("sec", "fld"), split_axis=2, concat_axis=0, tiled=True)
-    per_dev = slots_all // groups
-    state = columns.reshape(n_sec, n_fld, lev_s, per_dev)
-    state = jnp.transpose(state, (1, 0, 2, 3)).reshape(n_fld * n_sec * lev_s, per_dev)
-    gates = lax.dot_general(
-        source_weights, state, (((0,), (0,)), ((), ())), preferred_element_type=jnp.float32
-    )
-    spec_bands = inverses.shape[0]
-    flux_rows = inverses.shape[1]
-    source = jax.nn.softplus(gates).astype(jnp.bfloat16).reshape(spec_bands, flux_rows, per_dev)
-    flux = jnp.einsum("bpq,bqj->pj", inverses, source, preferred_element_type=jnp.float32)
-    band_place = lax.axis_index("band")
-    count = jnp.sum(
-        jnp.where(jnp.arange(n_band, dtype=jnp.int32) == band_place, counts, jnp.zeros_like(counts))
-    )
-    group_place = lax.axis_index(("sec", "fld"))
-    heat = heat_rates(flux, count, group_place * per_dev)
-    returned = lax.all_to_all(heat, ("sec", "fld"), split_axis=0, concat_axis=1, tiled=True)
-    spread = (
-        jnp.transpose(returned.astype(jnp.float32))[:, :, None]
-        * interp.astype(jnp.float32)[:, None, :]
-    )
-    spread_high = spread.astype(jnp.bfloat16)
-    spread_low = (spread - spread_high.astype(jnp.float32)).astype(jnp.bfloat16)
-    summed = lax.dot_general(
-        selector, spread_high, (((0,), (0,)), ((), ())), preferred_element_type=jnp.float32
-    )
-    summed = summed + lax.dot_general(
-        selector, spread_low, (((0,), (0,)), ((), ())), preferred_element_type=jnp.float32
-    )
-    return jnp.transpose(summed, (1, 0, 2)).reshape(returned.shape[0], lat_d, lon).astype(jnp.bfloat16)
-
-
-def body(grid, legendre, counts, blocks, interp, source_weights, inverses):
-    spectral = spectral_part(grid, legendre)
-    heating = heating_part(grid, counts, blocks, interp, source_weights, inverses)
     return (spectral, heating)
 
 

time: 95.2 us -> 68 us (0.71)
  starting transfers between devices: 13.2 us -> 0 us
  matrix products: 6.79 us -> 0 us
  other arithmetic: 6.44 us -> 0 us
  Pallas kernels: 53.2 us -> 59.4 us
  waiting for transfers between devices: 3.69 us -> 0 us
  local copies, waits for them, and re-layouts: 9.79 us -> 7.22 us
    all_to_all x2 -> x0, starting transfers between devices: 13.2 us -> none  [the longest x1 8.57 us: heating_part(): lax.all_to_all(partial_state, ('sec', 'fld'), split_axis=2, concat_axis=0...]
    dot_general x6 -> x0, matrix products: 6.79 us -> none  [the longest x1 2.39 us: heating_part(): lax.dot_general(selector, patch, (((1,), (1,)), ((), ())), preferred_elem...]
    pallas_call x1, Pallas kernels: 53.2 us -> 59.4 us  [body(): pl.pallas_call(kernel, out_shape=(jax.ShapeDtypeStruct((wave_dev, 2, n_fl...]
    reshape x3 -> x0, local copies, waits for them, and re-layouts: 4.01 us -> none  [the longest x1 3.62 us: heating_part(): patch = grid.reshape(lev_s, nblocks, width)]
    all_to_all x2 -> x0, waiting for transfers between devices: 3.69 us -> none  [the longest x1 3.69 us: heating_part(): lax.all_to_all(partial_state, ('sec', 'fld'), split_axis=2, concat_axis=0...]
    unnamed x20 -> x14, local copies, waits for them, and re-layouts: 3.72 us -> 7.22 us
    convert_element_type x2 -> x0, other arithmetic: 2.29 us -> none  [the longest x1 1.31 us: heat_rates(): return heat.astype(jnp.bfloat16)]
    unnamed x1 -> x0, other arithmetic: 2.27 us -> none
  transfers between devices with their start and end apart: 2 -> 0, of which waited for: 1 -> 0; matrix products, arithmetic and copies ran while one was open for 4% -> 0% of each run, Pallas kernels for 57% -> 0%
where the time goes in v2:
time: 68 us; the launch traced here: 67.3 us
  Pallas kernels  59.4 us (87%)
  local copies, waits for them, and re-layouts  7.22 us (11%)
    pallas_call x1, Pallas kernels, body(): pl.pallas_call(kernel, out_shape=(jax.ShapeDtypeStruct((wave_dev, 2, n_fl...  59.4 us
    unnamed x14, local copies, waits for them, and re-layouts  7.22 us

profile of v2, /device:TPU:32, one launch (start us, length us, event | category | flops | bytes accessed | tf_op | source)
XLA Modules:
  0.0 67.3 jit_solution(11206544496665500824)
XLA Ops:
  0.6 0.0 copy-start
  0.6 1.5 %copy-done = bf16[1,8,40,2688]{3,2,1,0:T(8,128)(2,1)S(1)} copy-done((bf16[1,8,40,2688]{3,2,1,0:T(8,128)(2,1)S(1)}, bf16[1,8,40,2688]{3,2,1,0:T(8,128)(2,1)}, u32[]{:S(2)}) %copy-start) | copy-done | bytes 1720344
  2.1 0.0 copy-start.1
  2.1 0.9 %copy-done.1 = bf16[1024,128]{1,0:T(8,128)(2,1)S(1)} copy-done((bf16[1024,128]{1,0:T(8,128)(2,1)S(1)}, bf16[1024,128]{1,0:T(8,128)(2,1)}, u32[]{:S(2)}) %copy-start.1) | copy-done | bytes 262168
  3.0 0.0 copy-start.2
  3.0 0.9 %copy-done.2 = bf16[64,2048]{1,0:T(8,128)(2,1)S(1)} copy-done((bf16[64,2048]{1,0:T(8,128)(2,1)S(1)}, bf16[64,2048]{1,0:T(8,128)(2,1)}, u32[]{:S(2)}) %copy-start.2) | copy-done | bytes 262168
  4.0 0.0 copy-start.3
  4.0 0.9 %copy-done.3 = bf16[64,32,32]{0,2,1:T(8,128)(2,1)S(1)} copy-done((bf16[64,32,32]{0,2,1:T(8,128)(2,1)S(1)}, bf16[64,32,32]{0,2,1:T(8,128)(2,1)}, u32[]{:S(2)}) %copy-start.3) | copy-done | bytes 131096
  4.9 0.0 copy-start.4
  4.9 0.7 %copy-done.4 = s32[1024]{0:T(1024)S(1)} copy-done((s32[1024]{0:T(1024)S(1)}, s32[1024]{0:T(1024)}, u32[]{:S(2)}) %copy-start.4) | copy-done | bytes 4120
  5.6 0.0 copy-start.5
  5.6 0.7 copy-done.5
  6.3 59.4 %shard_map.95 = (bf16[6,2,4,16,384]{4,3,2,1,0:T(8,128)(2,1)S(1)}, bf16[2,40,2688]{2,1,0:T(8,128)(2,1)S(1)}) custom-call(bf16[320,2688]{1,0:T(8,128)(2,1)S(1)} %bitcast.6, bf16[6,2688,256]{2,1,0:T(8,128)(2,1)} %constant.2.clone.tab_hbm, bf16[6,1280,384]{2,1,0:T(8,128)(2,1)} %leg_hbm.1, s32[1,32]{1,0:T(1,128)S(1)} %bitcast.9, s32[8,128]{1,0:T(8,128)S(1)} %bitcast.8, ...), custom_call_target="tpu_custom_call" | custom-call | tf_op jit(solution)/shard_map/pallas_call | solution.py:418
  65.7 0.8 %copy.12 = bf16[6,2,4,16,384]{4,3,2,1,0:T(8,128)(2,1)} copy(bf16[6,2,4,16,384]{4,3,2,1,0:T(8,128)(2,1)S(1)} %get-tuple-element.4) | data formatting | bytes 1179648
  66.5 0.8 %copy.13 = bf16[2,40,2688]{2,1,0:T(8,128)(2,1)} copy(bf16[2,40,2688]{2,1,0:T(8,128)(2,1)S(1)} %get-tuple-element.5) | data formatting | bytes 860160
Async XLA Ops:
  0.6 1.5 %copy-start = (bf16[1,8,40,2688]{3,2,1,0:T(8,128)(2,1)S(1)}, bf16[1,8,40,2688]{3,2,1,0:T(8,128)(2,1)}, u32[]{:S(2)}) copy-start(bf16[1,8,40,2688]{3,2,1,0:T(8,128)(2,1)} %param.8) | copy-start | bytes 5160964
  2.1 0.9 %copy-start.1 = (bf16[1024,128]{1,0:T(8,128)(2,1)S(1)}, bf16[1024,128]{1,0:T(8,128)(2,1)}, u32[]{:S(2)}) copy-start(bf16[1024,128]{1,0:T(8,128)(2,1)} %interp_hbm.1) | copy-start | bytes 786436
  3.0 0.9 %copy-start.2 = (bf16[64,2048]{1,0:T(8,128)(2,1)S(1)}, bf16[64,2048]{1,0:T(8,128)(2,1)}, u32[]{:S(2)}) copy-start(bf16[64,2048]{1,0:T(8,128)(2,1)} %weights_hbm.1) | copy-start | bytes 786436
  4.0 0.9 %copy-start.3 = (bf16[64,32,32]{0,2,1:T(8,128)(2,1)S(1)}, bf16[64,32,32]{0,2,1:T(8,128)(2,1)}, u32[]{:S(2)}) copy-start(bf16[64,32,32]{0,2,1:T(8,128)(2,1)} %param.14) | copy-start | bytes 393220
  4.9 0.7 %copy-start.4 = (s32[1024]{0:T(1024)S(1)}, s32[1024]{0:T(1024)}, u32[]{:S(2)}) copy-start(s32[1024]{0:T(1024)} %param.11) | copy-start | bytes 12292
  5.6 0.7 copy-start.5

commit v3 on v2

--- a/solution.py
+++ b/solution.py
@@ -55,7 +55,7 @@
     out_ref, heat_ref,
     g, tab, leg, send, recv, zsend, zrecv,
     counts, blocks, interp, weights, inverse,
-    ids, patch, inverse_wide, source, state_send, state_recv, heat_send, heat_recv,
+    ids, patch, hot, inverse_wide, source, state_send, state_recv, heat_send, heat_recv,
     load_sem, bs_sem, br_sem, zs_sem, zr_sem, rs_sem, rr_sem, small_sem, col_sem,
 ):
     lat = send.shape[2]
@@ -77,10 +77,10 @@
             leg_hbm.at[pl.ds(2 * c, 2)], leg.at[pl.ds(2 * c, 2)], load_sem.at[7 + c]
         )
 
-    half0 = band // 16
     load_g = pltpu.make_async_copy(grid_hbm, g, load_sem.at[6])
     load_g.start()
-    load_tab(half0).start()
+    load_tab(0).start()
+    load_tab(1).start()
 
     barrier = pltpu.get_barrier_semaphore()
 
@@ -93,51 +93,8 @@
     lax.fori_loop(1, N_BAND, greet, 0)
     for d in range(1, N_Z):
         pl.semaphore_signal(barrier, inc=1, device_id=zdev(d)[1], device_id_type=MESH)
-    load_g.wait()
-    pl.semaphore_wait(barrier, N_BAND - 1 + N_Z - 1)
-
-    def band_copy(c, to):
-        return pltpu.make_async_remote_copy(
-            src_ref=send.at[c, to],
-            dst_ref=recv.at[c, band],
-            send_sem=bs_sem.at[c],
-            recv_sem=br_sem.at[c],
-            device_id={"band": to},
-            device_id_type=MESH,
-        )
-
-    def table_of(t):
-        return (t // 2) * 2 + lax.rem(t + half0, 2)
-
-    def dft_step(t, _):
-        c = t // 2
-        half = lax.rem(t + half0, 2)
-
-        @pl.when(t < 5)
-        def _():
-            load_tab(table_of(t + 1)).start()
-
-        load_tab(table_of(t)).wait()
-        coeffs = jnp.dot(g[...], tab[table_of(t)], preferred_element_type=jnp.float32)
-        for tile in range(2):
-            rows = [coeffs[l * lat:(l + 1) * lat, tile * 128:(tile + 1) * 128] for l in range(8)]
-            rows = transpose_levels(rows)
-            for i in range(8):
-                send[c, half * 16 + tile * 8 + i] = rows[i].astype(jnp.bfloat16)
-
-        def send_one(k, _):
-            to = half * 16 + lax.rem(band + k, 16)
-
-            @pl.when(to != band)
-            def _():
-                band_copy(c, to).start()
-
-            return 0
-
-        lax.fori_loop(0, 16, send_one, 0)
-        return 0
-
-    lax.fori_loop(0, 2 * CHUNKS, dft_step, 0)
+    for t in range(2, 2 * CHUNKS):
+        load_tab(t).start()
     small = [
         pltpu.make_async_copy(source_ref, target_ref, small_sem.at[i])
         for i, (source_ref, target_ref) in enumerate(
@@ -145,10 +102,37 @@
              (inverse_hbm, inverse), (counts_hbm, counts))
         )
     ]
-    for load in small:
-        load.start()
-    for c in range(CHUNKS):
-        load_leg(c).start()
+    load_g.wait()
+
+    def dft_step(t, _):
+        c = t // 2
+        load_tab(t).wait()
+        coeffs = jnp.dot(g[...], tab[t], preferred_element_type=jnp.float32)
+        for tile in range(2):
+            rows = [coeffs[l * lat:(l + 1) * lat, tile * 128:(tile + 1) * 128] for l in range(8)]
+            rows = transpose_levels(rows)
+            for i in range(8):
+                send[c, lax.rem(t, 2) * 16 + tile * 8 + i] = rows[i].astype(jnp.bfloat16)
+        return 0
+
+    def dft(c):
+        lax.fori_loop(2 * c, 2 * c + 2, dft_step, 0)
+
+    def send_bands(c):
+        def one(k, _):
+            to = lax.rem(band + k, N_BAND)
+            pltpu.make_async_remote_copy(
+                src_ref=send.at[c, to],
+                dst_ref=recv.at[c, band],
+                send_sem=bs_sem.at[c],
+                recv_sem=br_sem.at[c],
+                device_id={"band": to},
+                device_id_type=MESH,
+            ).start()
+            return 0
+
+        lax.fori_loop(1, N_BAND, one, 0)
+        recv[c, band] = send[c, band]
 
     row = lax.broadcasted_iota(jnp.int32, (128, 128), 0)
     col = lax.broadcasted_iota(jnp.int32, (128, 128), 1)
@@ -178,7 +162,6 @@
         )
 
     def turn(c):
-        recv[c, band] = send[c, band]
         got = recv.at[c, pl.ds(0, N_BAND - 1)]
         pltpu.make_async_copy(got, got, br_sem.at[c]).wait()
         half = N_BAND // 2
@@ -263,42 +246,47 @@
     def gather_state():
         small[1].wait()
         lane = lax.broadcasted_iota(jnp.int32, (128, 128), 1)
-        level_of = lax.broadcasted_iota(jnp.int32, (8, 1024), 1) // 128
-        ones = (lax.broadcasted_iota(jnp.int32, (8, 1024), 0) == level_of).astype(jnp.bfloat16)
-
-        def one(k, _):
-            to = lax.rem(z + k, N_Z)
-            want = jnp.transpose(jnp.broadcast_to(ids[pl.ds(to, 1), :], (128, 128)))
-            hot = jnp.concatenate(
-                [(want == (lane + 128 * i).astype(jnp.float32)).astype(jnp.bfloat16)
-                 for i in range(PATCH_ROWS // 128)],
-                axis=1,
-            )
-            picked = jnp.dot(hot, patch[...], preferred_element_type=jnp.float32)
-            slot = pl.ds(pl.multiple_of(to * 128, 128), 128)
-            factor = interp[slot, :].astype(jnp.float32)
-            terms = picked * jnp.concatenate([factor] * 8, axis=1)
-            high = terms.astype(jnp.bfloat16)
-            low = (terms - high.astype(jnp.float32)).astype(jnp.bfloat16)
-            contract = (((1,), (1,)), ((), ()))
-            state_send[to] = lax.dot_general(
-                ones, high, contract, preferred_element_type=jnp.float32
-            ) + lax.dot_general(ones, low, contract, preferred_element_type=jnp.float32)
-
-            @pl.when(to != z)
-            def _():
-                column_copy(0, to, state_send, state_recv).start()
-
-            return 0
-
-        lax.fori_loop(1, N_Z + 1, one, 0)
-
-    def solve_columns():
+        row8 = lax.broadcasted_iota(jnp.int32, (8, 256), 0)
+        level_of = lax.broadcasted_iota(jnp.int32, (8, 256), 1) // 128
+        contract = (((1,), (1,)), ((), ()))
+        for half in range(2):
+            for k in range(4):
+                place = half * 4 + k
+                want = jnp.transpose(jnp.broadcast_to(ids[place:place + 1, :], (128, 128)))
+                hot[k * 128:(k + 1) * 128, :] = jnp.concatenate(
+                    [(want == (lane + 128 * i).astype(jnp.float32)).astype(jnp.bfloat16)
+                     for i in range(PATCH_ROWS // 128)],
+                    axis=1,
+                )
+
+            def two_levels(p, total):
+                cols = pl.ds(pl.multiple_of(p * 256, 256), 256)
+                picked = jnp.dot(hot[...], patch[:, cols], preferred_element_type=jnp.float32)
+                factor = interp[half * 512:(half + 1) * 512, :].astype(jnp.float32)
+                terms = picked * jnp.concatenate([factor, factor], axis=1)
+                high = terms.astype(jnp.bfloat16)
+                low = (terms - high.astype(jnp.float32)).astype(jnp.bfloat16)
+                ones = (row8 == level_of + 2 * p).astype(jnp.bfloat16)
+                return total + lax.dot_general(
+                    ones, high, contract, preferred_element_type=jnp.float32
+                ) + lax.dot_general(ones, low, contract, preferred_element_type=jnp.float32)
+
+            total = lax.fori_loop(0, 4, two_levels, jnp.zeros((8, 512), jnp.float32))
+            for k in range(4):
+                state_send[half * 4 + k] = total[:, k * 128:(k + 1) * 128]
+
+        def send_state(k, _):
+            column_copy(0, lax.rem(z + k, N_Z), state_send, state_recv).start()
+            return 0
+
+        lax.fori_loop(1, N_Z, send_state, 0)
+        state_recv[z] = state_send[z]
         small[2].wait()
         small[3].wait()
         small[4].wait()
         inverse_wide[...] = inverse[...].astype(jnp.float32)
-        state_recv[z] = state_send[z]
+
+    def solve_columns():
         column_wait(0, 1, state_recv)
         state = state_recv[...].reshape(64, 128).astype(jnp.bfloat16)
 
@@ -314,12 +302,14 @@
         spec_bands = inverse.shape[1]
         flux_rows = inverse.shape[0] // 32
 
-        def fluxes(q, total):
+        sums = []
+        for q in range(flux_rows):
             factor = inverse_wide[pl.ds(q, 32, stride=32), :].astype(jnp.bfloat16)
             value = source[pl.ds(q, spec_bands, stride=32), :].astype(jnp.bfloat16)
-            return total + jnp.dot(factor, value, preferred_element_type=jnp.float32)
-
-        flux = lax.fori_loop(0, flux_rows, fluxes, jnp.zeros((32, 128), jnp.float32))
+            sums.append(jnp.dot(factor, value, preferred_element_type=jnp.float32))
+        while len(sums) > 1:
+            sums = [first + second for first, second in zip(sums[::2], sums[1::2])]
+        flux = sums[0]
         row16 = lax.broadcasted_iota(jnp.int32, (16, 128), 0)
 
         def drop(rows):
@@ -377,18 +367,29 @@
 
         lax.fori_loop(0, pairs, one, 0)
 
+    dft(0)
+    for load in small:
+        load.start()
+    for c in range(CHUNKS):
+        load_leg(c).start()
+    pl.semaphore_wait(barrier, N_BAND - 1 + N_Z - 1)
+    send_bands(0)
+    dft(1)
+    send_bands(1)
+    block_patch()
+    gather_state()
     turn(0)
-    block_patch()
+    dft(2)
+    send_bands(2)
     turn(1)
-    gather_state()
     relay(0)
     turn(2)
     solve_columns()
     relay(1)
     legendre(0)
-    scatter_heat()
     relay(2)
     legendre(1)
+    scatter_heat()
     legendre(2)
 
     column_wait(0, 0, state_send)
@@ -418,10 +419,10 @@
     spectral, heating = pl.pallas_call(
         kernel,
         out_shape=(
-            jax.ShapeDtypeStruct((wave_dev, 2, n_fld, n_sec * lev_s, degrees), bf16),
-            jax.ShapeDtypeStruct((lev_out, lat_d, lon), bf16),
+            pltpu.VMEM((wave_dev, 2, n_fld, n_sec * lev_s, degrees), bf16),
+            pltpu.VMEM((lev_out, lat_d, lon), bf16),
         ),
-        in_specs=[pl.BlockSpec(memory_space=pl.ANY)] * 8,
+        in_specs=[pl.BlockSpec(memory_space=pltpu.HBM)] * 8,
         out_specs=(
             pl.BlockSpec(memory_space=pltpu.VMEM),
             pl.BlockSpec(memory_space=pltpu.VMEM),
@@ -441,6 +442,7 @@
             pltpu.VMEM(inv_rows.shape, bf16),
             pltpu.VMEM((N_Z, 128), f32),
             pltpu.VMEM((PATCH_ROWS, lev_s * width), bf16),
+            pltpu.VMEM((slots // 2, PATCH_ROWS), bf16),
             pltpu.VMEM(inv_rows.shape, f32),
             pltpu.VMEM((sources, 128), f32),
             pltpu.VMEM((N_Z, 8, 128), f32),
@@ -458,7 +460,7 @@
             pltpu.SemaphoreType.DMA((4,)),
         ],
         compiler_params=pltpu.CompilerParams(
-            collective_id=0, has_side_effects=True, vmem_limit_bytes=48 * 2**20
+            collective_id=0, has_side_effects=True, vmem_limit_bytes=62 * 2**20
         ),
     )(
         flat, table, legendre, counts.reshape(1, N_BAND), blocks.reshape(N_Z, 128), interp,

time: 68 us -> 59.2 us (0.87)
  local copies, waits for them, and re-layouts: 7.22 us -> 1.57 us
  Pallas kernels: 59.4 us -> 56.9 us
    unnamed x14 -> x2, local copies, waits for them, and re-layouts: 7.22 us -> 1.57 us
    pallas_call x1, Pallas kernels: 59.4 us -> 56.9 us  [body(): pl.pallas_call(kernel, out_shape=(pltpu.VMEM((wave_dev, 2, n_fld, n_sec *...]
where the time goes in v3:
time: 59.2 us; the launch traced here: 59.1 us
  Pallas kernels  56.9 us (96%)
  local copies, waits for them, and re-layouts  1.57 us (3%)
  between operations  0.64 us (1%)
    pallas_call x1, Pallas kernels, body(): pl.pallas_call(kernel, out_shape=(pltpu.VMEM((wave_dev, 2, n_fld, n_sec *...  56.9 us
    unnamed x2, local copies, waits for them, and re-layouts  1.57 us

profile of v3, /device:TPU:32, one launch (start us, length us, event | category | flops | bytes accessed | tf_op | source)
XLA Modules:
  0.0 59.1 jit_solution(8746993963575504174)
XLA Ops:
  0.6 56.9 %shard_map.95 = (bf16[6,2,4,16,384]{4,3,2,1,0:T(8,128)(2,1)S(1)}, bf16[2,40,2688]{2,1,0:T(8,128)(2,1)S(1)}) custom-call(bf16[320,2688]{1,0:T(8,128)(2,1)} %bitcast.6, bf16[6,2688,256]{2,1,0:T(8,128)(2,1)} %constant.2.clone.tab_hbm, bf16[6,1280,384]{2,1,0:T(8,128)(2,1)} %leg_hbm.1, s32[1,32]{1,0:T(1,128)} %bitcast.9, s32[8,128]{1,0:T(8,128)} %bitcast.8, ...), custom_call_target="tpu_custom_call" | custom-call | tf_op jit(solution)/shard_map/pallas_call | solution.py:419
  57.5 0.8 %copy.12 = bf16[6,2,4,16,384]{4,3,2,1,0:T(8,128)(2,1)} copy(bf16[6,2,4,16,384]{4,3,2,1,0:T(8,128)(2,1)S(1)} %get-tuple-element.2) | data formatting | bytes 1179648
  58.4 0.8 %copy.13 = bf16[2,40,2688]{2,1,0:T(8,128)(2,1)} copy(bf16[2,40,2688]{2,1,0:T(8,128)(2,1)S(1)} %get-tuple-element.3) | data formatting | bytes 860160

commit v4 on v3

--- a/solution.py
+++ b/solution.py
@@ -55,7 +55,7 @@
     out_ref, heat_ref,
     g, tab, leg, send, recv, zsend, zrecv,
     counts, blocks, interp, weights, inverse,
-    ids, patch, hot, inverse_wide, source, state_send, state_recv, heat_send, heat_recv,
+    ids, patch, patch_t, interp_t, inverse_wide, source, state_send, state_recv, heat_send, heat_recv,
     load_sem, bs_sem, br_sem, zs_sem, zr_sem, rs_sem, rr_sem, small_sem, col_sem,
 ):
     lat = send.shape[2]
@@ -172,9 +172,9 @@
                 preferred_element_type=jnp.float32,
             ).astype(jnp.bfloat16)
             zsend[c, :, :, part * half * lat:(part + 1) * half * lat] = turned.reshape(4, 32, half * lat)
-        for d in (3, 2, 1):
+        own_copy(c).start()
+        for d in (2, 3, 1):
             direct_copy(c, d).start()
-        own_copy(c).start()
         zrecv[c, z] = zsend[c, z // 2]
 
     def relay(c):
@@ -243,37 +243,40 @@
         part = buf.at[pl.ds(0, N_Z - 1)]
         pltpu.make_async_copy(part, part, col_sem.at[2 * kind + is_recv]).wait()
 
+    def turn_patch():
+        small[1].wait()
+
+        def one(i, _):
+            rows = pl.ds(pl.multiple_of(i * 128, 128), 128)
+            for l in range(8):
+                block = patch[rows, l * 128:(l + 1) * 128].astype(jnp.float32)
+                patch_t[l * 128:(l + 1) * 128, rows] = jnp.transpose(block).astype(jnp.bfloat16)
+            return 0
+
+        lax.fori_loop(0, PATCH_ROWS // 128, one, 0)
+        for place in range(N_Z):
+            span = slice(place * 128, (place + 1) * 128)
+            interp_t[:, span] = jnp.transpose(interp[span, :].astype(jnp.float32))
+
     def gather_state():
-        small[1].wait()
-        lane = lax.broadcasted_iota(jnp.int32, (128, 128), 1)
-        row8 = lax.broadcasted_iota(jnp.int32, (8, 256), 0)
-        level_of = lax.broadcasted_iota(jnp.int32, (8, 256), 1) // 128
-        contract = (((1,), (1,)), ((), ()))
-        for half in range(2):
-            for k in range(4):
-                place = half * 4 + k
-                want = jnp.transpose(jnp.broadcast_to(ids[place:place + 1, :], (128, 128)))
-                hot[k * 128:(k + 1) * 128, :] = jnp.concatenate(
-                    [(want == (lane + 128 * i).astype(jnp.float32)).astype(jnp.bfloat16)
-                     for i in range(PATCH_ROWS // 128)],
-                    axis=1,
-                )
-
-            def two_levels(p, total):
-                cols = pl.ds(pl.multiple_of(p * 256, 256), 256)
-                picked = jnp.dot(hot[...], patch[:, cols], preferred_element_type=jnp.float32)
-                factor = interp[half * 512:(half + 1) * 512, :].astype(jnp.float32)
-                terms = picked * jnp.concatenate([factor, factor], axis=1)
-                high = terms.astype(jnp.bfloat16)
-                low = (terms - high.astype(jnp.float32)).astype(jnp.bfloat16)
-                ones = (row8 == level_of + 2 * p).astype(jnp.bfloat16)
-                return total + lax.dot_general(
-                    ones, high, contract, preferred_element_type=jnp.float32
-                ) + lax.dot_general(ones, low, contract, preferred_element_type=jnp.float32)
-
-            total = lax.fori_loop(0, 4, two_levels, jnp.zeros((8, 512), jnp.float32))
-            for k in range(4):
-                state_send[half * 4 + k] = total[:, k * 128:(k + 1) * 128]
+        row = lax.broadcasted_iota(jnp.int32, (PATCH_ROWS, 128), 0).astype(jnp.float32)
+
+        def one(i, _):
+            hot = jnp.concatenate(
+                [(ids[pl.ds(2 * i + k, 1), :] == row).astype(jnp.bfloat16) for k in range(2)], axis=1
+            )
+            picked = jnp.dot(patch_t[...], hot, preferred_element_type=jnp.float32)
+            factor = interp_t[:, pl.ds(pl.multiple_of(i * 256, 256), 256)]
+            sums = [
+                jnp.sum(picked[l * 128:(l + 1) * 128] * factor, axis=0, keepdims=True)
+                for l in range(8)
+            ]
+            level = jnp.concatenate(sums, axis=0)
+            for k in range(2):
+                state_send[2 * i + k] = level[:, k * 128:(k + 1) * 128]
+            return 0
+
+        lax.fori_loop(0, N_Z // 2, one, 0)
 
         def send_state(k, _):
             column_copy(0, lax.rem(z + k, N_Z), state_send, state_recv).start()
@@ -377,6 +380,7 @@
     dft(1)
     send_bands(1)
     block_patch()
+    turn_patch()
     gather_state()
     turn(0)
     dft(2)
@@ -442,7 +446,8 @@
             pltpu.VMEM(inv_rows.shape, bf16),
             pltpu.VMEM((N_Z, 128), f32),
             pltpu.VMEM((PATCH_ROWS, lev_s * width), bf16),
-            pltpu.VMEM((slots // 2, PATCH_ROWS), bf16),
+            pltpu.VMEM((lev_s * width, PATCH_ROWS), bf16),
+            pltpu.VMEM((width, slots), f32),
             pltpu.VMEM(inv_rows.shape, f32),
             pltpu.VMEM((sources, 128), f32),
             pltpu.VMEM((N_Z, 8, 128), f32),

time: 59.2 us -> 55.3 us (0.934)
  Pallas kernels: 56.9 us -> 52.9 us
    pallas_call x1, Pallas kernels: 56.9 us -> 52.9 us  [body(): pl.pallas_call(kernel, out_shape=(pltpu.VMEM((wave_dev, 2, n_fld, n_sec *...]
where the time goes in v4:
time: 55.3 us; the launch traced here: 55.1 us
  Pallas kernels  52.9 us (96%)
  local copies, waits for them, and re-layouts  1.57 us (3%)
  between operations  0.64 us (1%)
    pallas_call x1, Pallas kernels, body(): pl.pallas_call(kernel, out_shape=(pltpu.VMEM((wave_dev, 2, n_fld, n_sec *...  52.9 us
    unnamed x2, local copies, waits for them, and re-layouts  1.57 us

profile of v4, /device:TPU:32, one launch (start us, length us, event | category | flops | bytes accessed | tf_op | source)
XLA Modules:
  0.0 55.1 jit_solution(4425788462229853705)
XLA Ops:
  0.6 52.9 %shard_map.95 = (bf16[6,2,4,16,384]{4,3,2,1,0:T(8,128)(2,1)S(1)}, bf16[2,40,2688]{2,1,0:T(8,128)(2,1)S(1)}) custom-call(bf16[320,2688]{1,0:T(8,128)(2,1)} %bitcast.6, bf16[6,2688,256]{2,1,0:T(8,128)(2,1)} %constant.2.clone.tab_hbm, bf16[6,1280,384]{2,1,0:T(8,128)(2,1)} %leg_hbm.1, s32[1,32]{1,0:T(1,128)} %bitcast.9, s32[8,128]{1,0:T(8,128)} %bitcast.8, ...), custom_call_target="tpu_custom_call" | custom-call | tf_op jit(solution)/shard_map/pallas_call | solution.py:423
  53.5 0.8 %copy.12 = bf16[6,2,4,16,384]{4,3,2,1,0:T(8,128)(2,1)} copy(bf16[6,2,4,16,384]{4,3,2,1,0:T(8,128)(2,1)S(1)} %get-tuple-element.2) | data formatting | bytes 1179648
  54.3 0.8 %copy.13 = bf16[2,40,2688]{2,1,0:T(8,128)(2,1)} copy(bf16[2,40,2688]{2,1,0:T(8,128)(2,1)S(1)} %get-tuple-element.3) | data formatting | bytes 860160

commit v5 on v4

--- a/solution.py
+++ b/solution.py
@@ -80,7 +80,6 @@
     load_g = pltpu.make_async_copy(grid_hbm, g, load_sem.at[6])
     load_g.start()
     load_tab(0).start()
-    load_tab(1).start()
 
     barrier = pltpu.get_barrier_semaphore()
 
@@ -93,8 +92,7 @@
     lax.fori_loop(1, N_BAND, greet, 0)
     for d in range(1, N_Z):
         pl.semaphore_signal(barrier, inc=1, device_id=zdev(d)[1], device_id_type=MESH)
-    for t in range(2, 2 * CHUNKS):
-        load_tab(t).start()
+    load_tab(1).start()
     small = [
         pltpu.make_async_copy(source_ref, target_ref, small_sem.at[i])
         for i, (source_ref, target_ref) in enumerate(
@@ -107,6 +105,11 @@
     def dft_step(t, _):
         c = t // 2
         load_tab(t).wait()
+
+        @pl.when(t < 2 * CHUNKS - 2)
+        def _():
+            load_tab(t + 2).start()
+
         coeffs = jnp.dot(g[...], tab[t], preferred_element_type=jnp.float32)
         for tile in range(2):
             rows = [coeffs[l * lat:(l + 1) * lat, tile * 128:(tile + 1) * 128] for l in range(8)]

time: 55.3 us -> 55.3 us (level)
  no operation moved by 1% of the time
where the time goes in v5:
time: 55.3 us; the launch traced here: 55.1 us
  Pallas kernels  52.9 us (96%)
  local copies, waits for them, and re-layouts  1.57 us (3%)
  between operations  0.64 us (1%)
    pallas_call x1, Pallas kernels, body(): pl.pallas_call(kernel, out_shape=(pltpu.VMEM((wave_dev, 2, n_fld, n_sec *...  52.9 us
    unnamed x2, local copies, waits for them, and re-layouts  1.57 us

profile of v5, /device:TPU:32, one launch (start us, length us, event | category | flops | bytes accessed | tf_op | source)
XLA Modules:
  0.0 55.1 jit_solution(279285702065349379)
XLA Ops:
  0.6 52.9 %shard_map.95 = (bf16[6,2,4,16,384]{4,3,2,1,0:T(8,128)(2,1)S(1)}, bf16[2,40,2688]{2,1,0:T(8,128)(2,1)S(1)}) custom-call(bf16[320,2688]{1,0:T(8,128)(2,1)} %bitcast.6, bf16[6,2688,256]{2,1,0:T(8,128)(2,1)} %constant.2.clone.tab_hbm, bf16[6,1280,384]{2,1,0:T(8,128)(2,1)} %leg_hbm.1, s32[1,32]{1,0:T(1,128)} %bitcast.9, s32[8,128]{1,0:T(8,128)} %bitcast.8, ...), custom_call_target="tpu_custom_call" | custom-call | tf_op jit(solution)/shard_map/pallas_call | solution.py:426
  53.5 0.8 %copy.12 = bf16[6,2,4,16,384]{4,3,2,1,0:T(8,128)(2,1)} copy(bf16[6,2,4,16,384]{4,3,2,1,0:T(8,128)(2,1)S(1)} %get-tuple-element.2) | data formatting | bytes 1179648
  54.4 0.8 %copy.13 = bf16[2,40,2688]{2,1,0:T(8,128)(2,1)} copy(bf16[2,40,2688]{2,1,0:T(8,128)(2,1)S(1)} %get-tuple-element.3) | data formatting | bytes 860160
